TPU v7x, 128 devices: a whole 4x4x4 slice. The times are simulated.
128 devices in a mesh: replica: 16 (over z_hi, y, core), shard: 8 (over x, z_lo).
Axes of the slice: x: 4, y: 4, z: 4 (z_hi: 2, z_lo: 2; z = z_hi * 2 + z_lo), core: 2. Of those that a mesh axis runs over, the one named last changes fastest.
Arguments:
- student_ctx: bfloat16 [163840, 1536], P(('replica', 'shard')), may hold values from -24 to 24
- out_grad: bfloat16 [163840, 1536], P(('replica', 'shard')), may hold values from -0.015625 to 0.015625
- weight: float32 [1536, 1536], P('shard'), may hold values from -0.15625 to 0.15625
- moment_one: float32 [1536, 1536], P('shard'), may hold values from -6 to 6
- moment_two: float32 [1536, 1536], P('shard'), may hold values from 0.05 to 2
- teacher: float32 [1536, 1536], P('shard'), may hold values from -0.15625 to 0.15625
- teach_input: bfloat16 [65536, 1536], P(('replica', 'shard')), may hold values from -6 to 6
- teach_ctx: bfloat16 [65536, 1536], P(('replica', 'shard')), may hold values from -6 to 6
Outputs:
- ctx_grad: bfloat16 [163840, 1536], P(('replica', 'shard'))
- weight_next: float32 [1536, 1536], P('shard')
- moment_one_next: float32 [1536, 1536], P('shard')
- moment_two_next: float32 [1536, 1536], P('shard')
- teacher_next: float32 [1536, 1536], P('shard')
- teacher_out: bfloat16 [65536, 1536], P(('replica', 'shard'))
All inputs are finite; a program needn't handle non-finite values.
Results may differ from a plain program's by a relative error of at most 0.0043.
The roundings to bfloat16 on the way count: a program that leaves them out, or rounds other values in their place, can miss the bound.
Values may be sent and summed in bfloat16 or wider, within the bound.
A program may use at most 192 MiB of HBM per device.

v0:
```python
import jax
import jax.numpy as jnp
from jax import lax
from jax.sharding import PartitionSpec as P

STEP = 100


beta_one = 0.9
beta_two = 0.999
adam_eps = 1e-08
learn_rate = 0.001
decay_rate = 0.04
momentum = 0.994


def body(student_ctx, out_grad, weight, moment_one, moment_two, teacher, teach_input, teach_ctx):
    features = weight.shape[1]
    token_count = student_ctx.shape[0]
    weight_half = weight.astype(jnp.bfloat16)
    teacher_next = momentum * teacher + (1.0 - momentum) * weight
    teacher_half = teacher_next.astype(jnp.bfloat16)
    columns = teach_ctx
    projected = jnp.dot(
        columns,
        lax.all_gather(teacher_half, "shard", axis=0, tiled=True),
        preferred_element_type=jnp.float32,
    )
    teacher_out = (teach_input.astype(jnp.float32) + projected).astype(jnp.bfloat16)
    product = lax.dot_general(
        out_grad,
        lax.all_gather(weight_half, "shard", axis=0, tiled=True),
        (((1,), (1,)), ((), ())),
        preferred_element_type=jnp.float32,
    )
    ctx_grad = product.astype(jnp.bfloat16)
    n_copies = lax.axis_size("replica")
    n_groups = lax.axis_size("shard")
    block_rows = features // (n_copies * n_groups)
    virtual_ctx = student_ctx.reshape(token_count, n_groups, n_copies, block_rows)
    virtual_ctx = virtual_ctx.transpose(0, 2, 1, 3).reshape(token_count, features)
    columns = virtual_ctx
    own_block = lax.psum_scatter(
        lax.dot_general(
            columns, out_grad, (((0,), (0,)), ((), ())), preferred_element_type=jnp.float32
        ),
        ("replica", "shard"),
        scatter_dimension=0,
        tiled=True,
    )
    gradient = lax.all_gather(own_block.astype(jnp.bfloat16), "replica", axis=0, tiled=True).astype(
        own_block.dtype
    )
    moment_one_next = beta_one * moment_one + (1.0 - beta_one) * gradient
    moment_two_next = beta_two * moment_two + (1.0 - beta_two) * gradient * gradient
    correct_one = 1.0 - beta_one**STEP
    correct_two = 1.0 - beta_two**STEP
    update = (
        moment_one_next / correct_one / (jnp.sqrt(moment_two_next / correct_two) + adam_eps)
        + decay_rate * weight
    )
    weight_next = weight - learn_rate * update
    return (ctx_grad, weight_next, moment_one_next, moment_two_next, teacher_next, teacher_out)


def solution(mesh):
    return jax.shard_map(
        body,
        mesh=mesh,
        in_specs=(
            P(("replica", "shard"), None),
            P(("replica", "shard"), None),
            P("shard", None),
            P("shard", None),
            P("shard", None),
            P("shard", None),
            P(("replica", "shard"), None),
            P(("replica", "shard"), None),
        ),
        out_specs=(
            P(("replica", "shard"), None),
            P("shard", None),
            P("shard", None),
            P("shard", None),
            P("shard", None),
            P(("replica", "shard"), None),
        ),
        check_vma=False,
    )
```

profile of v0, /device:TPU:0, one launch (start us, length us, event | category | flops | bytes accessed | tf_op | source)
XLA Modules:
  0.0 781.8 jit_solution(11342597224027583799)
XLA Ops:
  7.2 0.0 copy-start
  7.2 0.0 all-gather.6.cloned.1.call-start
  7.2 6.4 copy.20
  13.6 6.9 reshape.18
  20.5 5.5 copy.21
  26.0 7.0 reshape.19
  33.0 11.5 %fusion.8 = f32[1536,1536]{1,0:T(8,128)} fusion(bf16[1280,1536]{0,1:T(8,128)(2,1)} %reshape.19, bf16[1280,1536]{1,0:T(8,128)(2,1)} %param.9), kind=kOutput, calls=%fused_computation.13 | convolution fusion | flops 6039797760 | bytes 17301504 | tf_op jit(solution)/shard_map/dot_general | solution.py:44
  44.5 377.4 %fusion = f32[16,1536]{1,0:T(8,128)S(1)} fusion(f32[1536,1536]{1,0:T(8,128)} %fusion.8), kind=kCustom, calls=%all-reduce-scatter | all-reduce-scatter fusion | flops 3145729 | bytes 9535488
  421.9 1.3 collective-permute-start.30
  423.3 1.3 collective-permute-start.31
  424.6 1.3 collective-permute-start.29
  425.9 1.3 collective-permute-start.28
  427.2 1.3 collective-permute-start.27
  428.5 0.0 collective-permute-done.31
  428.5 1.3 collective-permute-start.26
  429.8 1.3 collective-permute-start.25
  431.1 1.3 collective-permute-start.24
  432.4 1.3 collective-permute-start.23
  433.7 12.2 %collective-permute-start.22 = (bf16[16,1536]{1,0:T(8,128)(2,1)S(1)}, bf16[16,1536]{1,0:T(8,128)(2,1)S(1)}, u32[]{:S(2)}, u32[]{:S(2)}) collective-permute-start(bf16[16,1536]{1,0:T(8,128)(2,1)S(1)} %convert.62), channel_id=1, source_target_pairs={{0,23},{1,24},{2,25},{3,26},{4,27},{5,28},{6,29},{7,30},{8,31},{9,... | collective-permute-start | bytes 147464
  445.9 0.0 copy-start.1
  445.9 4.7 collective-permute-start.21
  450.7 0.0 copy-start.2
  450.7 3.5 collective-permute-start.20
  454.2 0.0 copy-start.3
  454.2 2.5 collective-permute-start.19
  456.7 0.0 copy-start.4
  456.8 1.3 collective-permute-start.18
  458.1 0.0 copy-start.5
  458.1 1.3 collective-permute-start.17
  459.4 0.0 copy-start.6
  459.4 4.7 collective-permute-start.16
  464.2 1.3 collective-permute-start.15
  465.5 3.5 collective-permute-start.14
  469.0 2.2 collective-permute-start.13
  471.2 2.5 collective-permute-start.12
  473.7 2.8 collective-permute-start.11
  476.5 3.3 collective-permute-start.10
  479.9 1.3 collective-permute-start.9
  481.2 2.9 collective-permute-start.8
  484.2 2.8 collective-permute-start.7
  487.0 3.7 collective-permute-start.6
  490.8 2.1 collective-permute-start.5
  492.9 2.8 collective-permute-start.4
  495.7 4.3 collective-permute-start.3
  500.1 1.3 collective-permute-start.2
  501.4 2.8 collective-permute-start.1
  504.2 4.6 collective-permute-start
  509.1 0.4 copy-done.23
  509.4 0.0 copy-done.24
  509.4 0.0 copy-done.25
  509.5 0.6 copy-done.26
  510.1 26.0 %concatenate = bf16[524,1536]{1,0:T(8,128)(2,1)S(1)} concatenate(bf16[12,1536]{1,0:T(8,128)(2,1)S(1)} %collective-permute-done.31, bf16[16,1536]{1,0:T(8,128)(2,1)S(1)} %collective-permute-done.30, bf16[16,1536]{1,0:T(8,128)(2,1)S(1)} %collective-permute-done.29, bf16[16,1536]{1,0:T(8,128)(2,1)S(1)} %collective-permute-done.28, bf16[16,1536]{1,0:T(8,128)(2,1)S(1)} %collective-permute-done.27, ...), dimensions={0} | concatenate | bytes 3268608
  536.1 23.2 %all-gather = bf16[16,12,1536]{2,1,0:T(8,128)(2,1)S(1)} all-gather(bf16[1,12,1536]{2,1,0:T(8,128)(2,1)S(1)} %fusion.4), channel_id=1, replica_groups=mesh['replica'=16,'shard'=8] {'replica'}, dimensions={0}, use_global_device_ids=true | all-gather | bytes 626688 | tf_op jit(solution)/shard_map/all_gather | solution.py:51
  559.3 0.1 reshape.22
  559.4 5.6 fusion.5
  564.9 0.0 all-gather.6.cloned.1.call-update
  565.0 0.2 all-gather.4.cloned.1.call-start
  565.2 0.5 all-gather.4.cloned.1.call-update
  565.7 1.7 copy.22
  567.5 94.7 %all-gather.6.cloned.1.call-done = bf16[1536,1536]{1,0:T(8,128)(2,1)} async-done(((bf16[192,1536]{1,0:T(8,128)(2,1)}), bf16[1536,1536]{1,0:T(8,128)(2,1)}) %all-gather.6.cloned.1.call-update) | async-done | bytes 4718608 | tf_op jit(solution)/shard_map/all_gather | solution.py:26
  662.1 6.1 fusion.2
  668.3 2.6 copy.23
  670.8 93.5 %all-gather.4.cloned.1.call-done = bf16[1536,1536]{1,0:T(8,128)(2,1)} async-done(((bf16[192,1536]{1,0:T(8,128)(2,1)}), bf16[1536,1536]{1,0:T(8,128)(2,1)}) %all-gather.4.cloned.1.call-update) | async-done | bytes 4718608 | tf_op jit(solution)/shard_map/all_gather | solution.py:32
  764.4 10.6 %convolution_convert_fusion = bf16[1280,1536]{1,0:T(8,128)(2,1)} fusion(bf16[1280,1536]{1,0:T(8,128)(2,1)} %param.9, bf16[1536,1536]{1,0:T(8,128)(2,1)} %all-gather.4.cloned.1.call-done), kind=kOutput, calls=%fused_computation | convolution fusion | flops 6041763840 | bytes 12582912 | tf_op jit(solution)/shard_map/dot_general | solution.py:30
  (77 shorter events, 0.2 us)
Async XLA Ops:
  7.2 654.9 %copy-start = (bf16[512,1536]{1,0:T(8,128)(2,1)S(1)}, bf16[512,1536]{1,0:T(8,128)(2,1)}, u32[]{:S(2)}) copy-start(bf16[512,1536]{1,0:T(8,128)(2,1)} %param.15) | copy-start | bytes 4718596
  7.2 654.9 %all-gather.6.cloned.1.call-start = ((), (), s32[]{:S(2)}) async-start(), calls=%async_computation.1 | async-start | bytes 5308416 | tf_op jit(solution)/shard_map/all_gather | solution.py:26
  421.9 7.8 %collective-permute-start.30 = (bf16[16,1536]{1,0:T(8,128)(2,1)S(1)}, bf16[16,1536]{1,0:T(8,128)(2,1)S(1)}, u32[]{:S(2)}, u32[]{:S(2)}) collective-permute-start(bf16[16,1536]{1,0:T(8,128)(2,1)S(1)} %convert.62), channel_id=1, source_target_pairs={{0,31},{1,32},{2,33},{3,34},{4,35},{5,36},{6,37},{7,38},{8,39},{9,... | collective-permute-start | bytes 147464
  423.3 5.2 collective-permute-start.31
  424.6 6.5 collective-permute-start.29
  425.9 6.5 collective-permute-start.28
  427.2 6.5 collective-permute-start.27
  428.5 17.4 %collective-permute-start.26 = (bf16[16,1536]{1,0:T(8,128)(2,1)S(1)}, bf16[16,1536]{1,0:T(8,128)(2,1)S(1)}, u32[]{:S(2)}, u32[]{:S(2)}) collective-permute-start(bf16[16,1536]{1,0:T(8,128)(2,1)S(1)} %convert.62), channel_id=1, source_target_pairs={{0,27},{1,28},{2,29},{3,30},{4,31},{5,32},{6,33},{7,34},{8,35},{9,... | collective-permute-start | bytes 147464
  429.8 20.9 %collective-permute-start.25 = (bf16[16,1536]{1,0:T(8,128)(2,1)S(1)}, bf16[16,1536]{1,0:T(8,128)(2,1)S(1)}, u32[]{:S(2)}, u32[]{:S(2)}) collective-permute-start(bf16[16,1536]{1,0:T(8,128)(2,1)S(1)} %convert.62), channel_id=1, source_target_pairs={{0,26},{1,27},{2,28},{3,29},{4,30},{5,31},{6,32},{7,33},{8,34},{9,... | collective-permute-start | bytes 147464
  431.1 23.1 %collective-permute-start.24 = (bf16[16,1536]{1,0:T(8,128)(2,1)S(1)}, bf16[16,1536]{1,0:T(8,128)(2,1)S(1)}, u32[]{:S(2)}, u32[]{:S(2)}) collective-permute-start(bf16[16,1536]{1,0:T(8,128)(2,1)S(1)} %convert.62), channel_id=1, source_target_pairs={{0,25},{1,26},{2,27},{3,28},{4,29},{5,30},{6,31},{7,32},{8,33},{9,... | collective-permute-start | bytes 147464
  432.4 24.3 %collective-permute-start.23 = (bf16[16,1536]{1,0:T(8,128)(2,1)S(1)}, bf16[16,1536]{1,0:T(8,128)(2,1)S(1)}, u32[]{:S(2)}, u32[]{:S(2)}) collective-permute-start(bf16[16,1536]{1,0:T(8,128)(2,1)S(1)} %convert.62), channel_id=1, source_target_pairs={{0,24},{1,25},{2,26},{3,27},{4,28},{5,29},{6,30},{7,31},{8,32},{9,... | collective-permute-start | bytes 147464
  433.7 24.3 %collective-permute-start.22 = (bf16[16,1536]{1,0:T(8,128)(2,1)S(1)}, bf16[16,1536]{1,0:T(8,128)(2,1)S(1)}, u32[]{:S(2)}, u32[]{:S(2)}) collective-permute-start(bf16[16,1536]{1,0:T(8,128)(2,1)S(1)} %convert.62), channel_id=1, source_target_pairs={{0,23},{1,24},{2,25},{3,26},{4,27},{5,28},{6,29},{7,30},{8,31},{9,... | collective-permute-start | bytes 147464
  445.9 63.0 %copy-start.1 = (bf16[16,1536]{1,0:T(8,128)(2,1)}, bf16[16,1536]{1,0:T(8,128)(2,1)S(1)}, u32[]{:S(2)}) copy-start(bf16[16,1536]{1,0:T(8,128)(2,1)S(1)} %collective-permute-done.26) | copy-start | bytes 147460
  445.9 13.5 %collective-permute-start.21 = (bf16[16,1536]{1,0:T(8,128)(2,1)S(1)}, bf16[16,1536]{1,0:T(8,128)(2,1)S(1)}, u32[]{:S(2)}, u32[]{:S(2)}) collective-permute-start(bf16[16,1536]{1,0:T(8,128)(2,1)S(1)} %convert.62), channel_id=1, source_target_pairs={{0,22},{1,23},{2,24},{3,25},{4,26},{5,27},{6,28},{7,29},{8,30},{9,... | collective-permute-start | bytes 147464
  450.7 58.2 %copy-start.2 = (bf16[16,1536]{1,0:T(8,128)(2,1)}, bf16[16,1536]{1,0:T(8,128)(2,1)S(1)}, u32[]{:S(2)}) copy-start(bf16[16,1536]{1,0:T(8,128)(2,1)S(1)} %collective-permute-done.25) | copy-start | bytes 147460
  450.7 13.5 %collective-permute-start.20 = (bf16[16,1536]{1,0:T(8,128)(2,1)S(1)}, bf16[16,1536]{1,0:T(8,128)(2,1)S(1)}, u32[]{:S(2)}, u32[]{:S(2)}) collective-permute-start(bf16[16,1536]{1,0:T(8,128)(2,1)S(1)} %convert.62), channel_id=1, source_target_pairs={{0,21},{1,22},{2,23},{3,24},{4,25},{5,26},{6,27},{7,28},{8,29},{9,... | collective-permute-start | bytes 147464
  454.2 54.7 %copy-start.3 = (bf16[16,1536]{1,0:T(8,128)(2,1)}, bf16[16,1536]{1,0:T(8,128)(2,1)S(1)}, u32[]{:S(2)}) copy-start(bf16[16,1536]{1,0:T(8,128)(2,1)S(1)} %collective-permute-done.24) | copy-start | bytes 147460
  454.2 11.3 %collective-permute-start.19 = (bf16[16,1536]{1,0:T(8,128)(2,1)S(1)}, bf16[16,1536]{1,0:T(8,128)(2,1)S(1)}, u32[]{:S(2)}, u32[]{:S(2)}) collective-permute-start(bf16[16,1536]{1,0:T(8,128)(2,1)S(1)} %convert.62), channel_id=1, source_target_pairs={{0,20},{1,21},{2,22},{3,23},{4,24},{5,25},{6,26},{7,27},{8,28},{9,... | collective-permute-start | bytes 147464
  456.7 52.1 %copy-start.4 = (bf16[16,1536]{1,0:T(8,128)(2,1)}, bf16[16,1536]{1,0:T(8,128)(2,1)S(1)}, u32[]{:S(2)}) copy-start(bf16[16,1536]{1,0:T(8,128)(2,1)S(1)} %collective-permute-done.23) | copy-start | bytes 147460
  456.8 12.2 %collective-permute-start.18 = (bf16[16,1536]{1,0:T(8,128)(2,1)S(1)}, bf16[16,1536]{1,0:T(8,128)(2,1)S(1)}, u32[]{:S(2)}, u32[]{:S(2)}) collective-permute-start(bf16[16,1536]{1,0:T(8,128)(2,1)S(1)} %convert.62), channel_id=1, source_target_pairs={{0,19},{1,20},{2,21},{3,22},{4,23},{5,24},{6,25},{7,26},{8,27},{9,... | collective-permute-start | bytes 147464
  458.1 50.8 %copy-start.5 = (bf16[16,1536]{1,0:T(8,128)(2,1)}, bf16[16,1536]{1,0:T(8,128)(2,1)S(1)}, u32[]{:S(2)}) copy-start(bf16[16,1536]{1,0:T(8,128)(2,1)S(1)} %collective-permute-done.22) | copy-start | bytes 147460
  458.1 13.1 %collective-permute-start.17 = (bf16[16,1536]{1,0:T(8,128)(2,1)S(1)}, bf16[16,1536]{1,0:T(8,128)(2,1)S(1)}, u32[]{:S(2)}, u32[]{:S(2)}) collective-permute-start(bf16[16,1536]{1,0:T(8,128)(2,1)S(1)} %convert.62), channel_id=1, source_target_pairs={{0,18},{1,19},{2,20},{3,21},{4,22},{5,23},{6,24},{7,25},{8,26},{9,... | collective-permute-start | bytes 147464
  459.4 49.5 %copy-start.6 = (bf16[16,1536]{1,0:T(8,128)(2,1)}, bf16[16,1536]{1,0:T(8,128)(2,1)S(1)}, u32[]{:S(2)}) copy-start(bf16[16,1536]{1,0:T(8,128)(2,1)S(1)} %collective-permute-done.21) | copy-start | bytes 147460
  459.4 14.3 %collective-permute-start.16 = (bf16[16,1536]{1,0:T(8,128)(2,1)S(1)}, bf16[16,1536]{1,0:T(8,128)(2,1)S(1)}, u32[]{:S(2)}, u32[]{:S(2)}) collective-permute-start(bf16[16,1536]{1,0:T(8,128)(2,1)S(1)} %convert.62), channel_id=1, source_target_pairs={{0,17},{1,18},{2,19},{3,20},{4,21},{5,22},{6,23},{7,24},{8,25},{9,... | collective-permute-start | bytes 147464
  464.2 44.7 %copy-start.7 = (bf16[16,1536]{1,0:T(8,128)(2,1)}, bf16[16,1536]{1,0:T(8,128)(2,1)S(1)}, u32[]{:S(2)}) copy-start(bf16[16,1536]{1,0:T(8,128)(2,1)S(1)} %collective-permute-done.20) | copy-start | bytes 147460
  464.2 12.3 %collective-permute-start.15 = (bf16[16,1536]{1,0:T(8,128)(2,1)S(1)}, bf16[16,1536]{1,0:T(8,128)(2,1)S(1)}, u32[]{:S(2)}, u32[]{:S(2)}) collective-permute-start(bf16[16,1536]{1,0:T(8,128)(2,1)S(1)} %convert.62), channel_id=1, source_target_pairs={{0,16},{1,17},{2,18},{3,19},{4,20},{5,21},{6,22},{7,23},{8,24},{9,... | collective-permute-start | bytes 147464
  465.5 43.4 %copy-start.8 = (bf16[16,1536]{1,0:T(8,128)(2,1)}, bf16[16,1536]{1,0:T(8,128)(2,1)S(1)}, u32[]{:S(2)}) copy-start(bf16[16,1536]{1,0:T(8,128)(2,1)S(1)} %collective-permute-done.19) | copy-start | bytes 147460
  465.5 14.4 %collective-permute-start.14 = (bf16[16,1536]{1,0:T(8,128)(2,1)S(1)}, bf16[16,1536]{1,0:T(8,128)(2,1)S(1)}, u32[]{:S(2)}, u32[]{:S(2)}) collective-permute-start(bf16[16,1536]{1,0:T(8,128)(2,1)S(1)} %convert.62), channel_id=1, source_target_pairs={{0,15},{1,16},{2,17},{3,18},{4,19},{5,20},{6,21},{7,22},{8,23},{9,... | collective-permute-start | bytes 147464
  469.0 40.0 %copy-start.9 = (bf16[16,1536]{1,0:T(8,128)(2,1)}, bf16[16,1536]{1,0:T(8,128)(2,1)S(1)}, u32[]{:S(2)}) copy-start(bf16[16,1536]{1,0:T(8,128)(2,1)S(1)} %collective-permute-done.18) | copy-start | bytes 147460
  469.0 12.2 %collective-permute-start.13 = (bf16[16,1536]{1,0:T(8,128)(2,1)S(1)}, bf16[16,1536]{1,0:T(8,128)(2,1)S(1)}, u32[]{:S(2)}, u32[]{:S(2)}) collective-permute-start(bf16[16,1536]{1,0:T(8,128)(2,1)S(1)} %convert.62), channel_id=1, source_target_pairs={{0,14},{1,15},{2,16},{3,17},{4,18},{5,19},{6,20},{7,21},{8,22},{9,... | collective-permute-start | bytes 147464
  471.2 37.7 %copy-start.10 = (bf16[16,1536]{1,0:T(8,128)(2,1)}, bf16[16,1536]{1,0:T(8,128)(2,1)S(1)}, u32[]{:S(2)}) copy-start(bf16[16,1536]{1,0:T(8,128)(2,1)S(1)} %collective-permute-done.17) | copy-start | bytes 147460
  471.2 12.9 %collective-permute-start.12 = (bf16[16,1536]{1,0:T(8,128)(2,1)S(1)}, bf16[16,1536]{1,0:T(8,128)(2,1)S(1)}, u32[]{:S(2)}, u32[]{:S(2)}) collective-permute-start(bf16[16,1536]{1,0:T(8,128)(2,1)S(1)} %convert.62), channel_id=1, source_target_pairs={{0,13},{1,14},{2,15},{3,16},{4,17},{5,18},{6,19},{7,20},{8,21},{9,... | collective-permute-start | bytes 147464
  473.7 35.2 %copy-start.11 = (bf16[16,1536]{1,0:T(8,128)(2,1)}, bf16[16,1536]{1,0:T(8,128)(2,1)S(1)}, u32[]{:S(2)}) copy-start(bf16[16,1536]{1,0:T(8,128)(2,1)S(1)} %collective-permute-done.16) | copy-start | bytes 147460
  473.7 13.3 %collective-permute-start.11 = (bf16[16,1536]{1,0:T(8,128)(2,1)S(1)}, bf16[16,1536]{1,0:T(8,128)(2,1)S(1)}, u32[]{:S(2)}, u32[]{:S(2)}) collective-permute-start(bf16[16,1536]{1,0:T(8,128)(2,1)S(1)} %convert.62), channel_id=1, source_target_pairs={{0,12},{1,13},{2,14},{3,15},{4,16},{5,17},{6,18},{7,19},{8,20},{9,... | collective-permute-start | bytes 147464
  476.5 32.4 %copy-start.12 = (bf16[16,1536]{1,0:T(8,128)(2,1)}, bf16[16,1536]{1,0:T(8,128)(2,1)S(1)}, u32[]{:S(2)}) copy-start(bf16[16,1536]{1,0:T(8,128)(2,1)S(1)} %collective-permute-done.15) | copy-start | bytes 147460
  476.5 14.3 %collective-permute-start.10 = (bf16[16,1536]{1,0:T(8,128)(2,1)S(1)}, bf16[16,1536]{1,0:T(8,128)(2,1)S(1)}, u32[]{:S(2)}, u32[]{:S(2)}) collective-permute-start(bf16[16,1536]{1,0:T(8,128)(2,1)S(1)} %convert.62), channel_id=1, source_target_pairs={{0,11},{1,12},{2,13},{3,14},{4,15},{5,16},{6,17},{7,18},{8,19},{9,... | collective-permute-start | bytes 147464
  479.9 29.1 %copy-start.13 = (bf16[16,1536]{1,0:T(8,128)(2,1)}, bf16[16,1536]{1,0:T(8,128)(2,1)S(1)}, u32[]{:S(2)}) copy-start(bf16[16,1536]{1,0:T(8,128)(2,1)S(1)} %collective-permute-done.14) | copy-start | bytes 147460
  479.9 13.0 %collective-permute-start.9 = (bf16[16,1536]{1,0:T(8,128)(2,1)S(1)}, bf16[16,1536]{1,0:T(8,128)(2,1)S(1)}, u32[]{:S(2)}, u32[]{:S(2)}) collective-permute-start(bf16[16,1536]{1,0:T(8,128)(2,1)S(1)} %convert.62), channel_id=1, source_target_pairs={{0,10},{1,11},{2,12},{3,13},{4,14},{5,15},{6,16},{7,17},{8,18},{9,... | collective-permute-start | bytes 147464
  481.2 27.8 %copy-start.14 = (bf16[16,1536]{1,0:T(8,128)(2,1)}, bf16[16,1536]{1,0:T(8,128)(2,1)S(1)}, u32[]{:S(2)}) copy-start(bf16[16,1536]{1,0:T(8,128)(2,1)S(1)} %collective-permute-done.13) | copy-start | bytes 147460
  481.2 14.5 %collective-permute-start.8 = (bf16[16,1536]{1,0:T(8,128)(2,1)S(1)}, bf16[16,1536]{1,0:T(8,128)(2,1)S(1)}, u32[]{:S(2)}, u32[]{:S(2)}) collective-permute-start(bf16[16,1536]{1,0:T(8,128)(2,1)S(1)} %convert.62), channel_id=1, source_target_pairs={{0,9},{1,10},{2,11},{3,12},{4,13},{5,14},{6,15},{7,16},{8,17},{9,1... | collective-permute-start | bytes 147464
  484.2 24.8 %copy-start.15 = (bf16[16,1536]{1,0:T(8,128)(2,1)}, bf16[16,1536]{1,0:T(8,128)(2,1)S(1)}, u32[]{:S(2)}) copy-start(bf16[16,1536]{1,0:T(8,128)(2,1)S(1)} %collective-permute-done.12) | copy-start | bytes 147460
  484.2 15.9 %collective-permute-start.7 = (bf16[16,1536]{1,0:T(8,128)(2,1)S(1)}, bf16[16,1536]{1,0:T(8,128)(2,1)S(1)}, u32[]{:S(2)}, u32[]{:S(2)}) collective-permute-start(bf16[16,1536]{1,0:T(8,128)(2,1)S(1)} %convert.62), channel_id=1, source_target_pairs={{0,8},{1,9},{2,10},{3,11},{4,12},{5,13},{6,14},{7,15},{8,16},{9,17... | collective-permute-start | bytes 147464
  487.0 22.0 %copy-start.16 = (bf16[16,1536]{1,0:T(8,128)(2,1)}, bf16[16,1536]{1,0:T(8,128)(2,1)S(1)}, u32[]{:S(2)}) copy-start(bf16[16,1536]{1,0:T(8,128)(2,1)S(1)} %collective-permute-done.11) | copy-start | bytes 147460
  487.0 14.3 %collective-permute-start.6 = (bf16[16,1536]{1,0:T(8,128)(2,1)S(1)}, bf16[16,1536]{1,0:T(8,128)(2,1)S(1)}, u32[]{:S(2)}, u32[]{:S(2)}) collective-permute-start(bf16[16,1536]{1,0:T(8,128)(2,1)S(1)} %convert.62), channel_id=1, source_target_pairs={{0,7},{1,8},{2,9},{3,10},{4,11},{5,12},{6,13},{7,14},{8,15},{9,16}... | collective-permute-start | bytes 147464
  490.8 18.2 %copy-start.17 = (bf16[16,1536]{1,0:T(8,128)(2,1)}, bf16[16,1536]{1,0:T(8,128)(2,1)S(1)}, u32[]{:S(2)}) copy-start(bf16[16,1536]{1,0:T(8,128)(2,1)S(1)} %collective-permute-done.10) | copy-start | bytes 147460
  490.8 13.4 %collective-permute-start.5 = (bf16[16,1536]{1,0:T(8,128)(2,1)S(1)}, bf16[16,1536]{1,0:T(8,128)(2,1)S(1)}, u32[]{:S(2)}, u32[]{:S(2)}) collective-permute-start(bf16[16,1536]{1,0:T(8,128)(2,1)S(1)} %convert.62), channel_id=1, source_target_pairs={{0,6},{1,7},{2,8},{3,9},{4,10},{5,11},{6,12},{7,13},{8,14},{9,15},... | collective-permute-start | bytes 147464
  492.9 16.1 %copy-start.18 = (bf16[16,1536]{1,0:T(8,128)(2,1)}, bf16[16,1536]{1,0:T(8,128)(2,1)S(1)}, u32[]{:S(2)}) copy-start(bf16[16,1536]{1,0:T(8,128)(2,1)S(1)} %collective-permute-done.9) | copy-start | bytes 147460
  492.9 15.9 %collective-permute-start.4 = (bf16[16,1536]{1,0:T(8,128)(2,1)S(1)}, bf16[16,1536]{1,0:T(8,128)(2,1)S(1)}, u32[]{:S(2)}, u32[]{:S(2)}) collective-permute-start(bf16[16,1536]{1,0:T(8,128)(2,1)S(1)} %convert.62), channel_id=1, source_target_pairs={{0,5},{1,6},{2,7},{3,8},{4,9},{5,10},{6,11},{7,12},{8,13},{9,14},{... | collective-permute-start | bytes 147464
  495.7 13.3 %copy-start.19 = (bf16[16,1536]{1,0:T(8,128)(2,1)}, bf16[16,1536]{1,0:T(8,128)(2,1)S(1)}, u32[]{:S(2)}) copy-start(bf16[16,1536]{1,0:T(8,128)(2,1)S(1)} %collective-permute-done.8) | copy-start | bytes 147460
  495.7 13.1 %collective-permute-start.3 = (bf16[16,1536]{1,0:T(8,128)(2,1)S(1)}, bf16[16,1536]{1,0:T(8,128)(2,1)S(1)}, u32[]{:S(2)}, u32[]{:S(2)}) collective-permute-start(bf16[16,1536]{1,0:T(8,128)(2,1)S(1)} %convert.62), channel_id=1, source_target_pairs={{0,4},{1,5},{2,6},{3,7},{4,8},{5,9},{6,10},{7,11},{8,12},{9,13},{1... | collective-permute-start | bytes 147464
  500.0 9.0 %copy-start.20 = (bf16[16,1536]{1,0:T(8,128)(2,1)}, bf16[16,1536]{1,0:T(8,128)(2,1)S(1)}, u32[]{:S(2)}) copy-start(bf16[16,1536]{1,0:T(8,128)(2,1)S(1)} %collective-permute-done.7) | copy-start | bytes 147460
  500.1 8.8 %collective-permute-start.2 = (bf16[16,1536]{1,0:T(8,128)(2,1)S(1)}, bf16[16,1536]{1,0:T(8,128)(2,1)S(1)}, u32[]{:S(2)}, u32[]{:S(2)}) collective-permute-start(bf16[16,1536]{1,0:T(8,128)(2,1)S(1)} %convert.62), channel_id=1, source_target_pairs={{0,3},{1,4},{2,5},{3,6},{4,7},{5,8},{6,9},{7,10},{8,11},{9,12},{10... | collective-permute-start | bytes 147464
  501.4 7.7 copy-start.21
  501.4 7.5 collective-permute-start.1
  504.2 4.8 copy-start.22
  504.2 5.9 collective-permute-start
  508.8 0.6 copy-start.23
  508.8 0.6 copy-start.24
  508.8 0.6 copy-start.25
  509.5 0.6 copy-start.26
  565.0 199.4 %all-gather.4.cloned.1.call-start = ((), (), s32[]{:S(2)}) async-start(), calls=%async_computation | async-start | bytes 5308416 | tf_op jit(solution)/shard_map/all_gather | solution.py:32
Sparse Core Ops, SparseCore 0:
  565.1 96.9 all-gather.5
  663.7 100.5 all-gather.3
where the time goes:
time: 786 us; the launch traced here: 782 us
  blocking collectives  401 us (51%)
  waiting for transfers between devices  189 us (24%)
  starting transfers between devices  86.3 us (11%)
  local copies, waits for them, and re-layouts  57.3 us (7%)
  matrix products  28.3 us (4%)
  between operations  14.9 us (2%)
    unnamed x1, blocking collectives  377 us
    all_gather x1, waiting for transfers between devices, body(): lax.all_gather(teacher_half, 'shard', axis=0, tiled=True)  94.7 us
    all_gather x1, waiting for transfers between devices, body(): lax.all_gather(weight_half, 'shard', axis=0, tiled=True)  93.5 us
    unnamed x32, starting transfers between devices  86.1 us
    unnamed x60, local copies, waits for them, and re-layouts  37.8 us
    all_gather x1, blocking collectives, body(): lax.all_gather(own_block.astype(jnp.bfloat16), 'replica', axis=0, tiled=T...  23.2 us
  transfers between devices with their start and end apart: 34, of which 2 were waited for; matrix products, arithmetic and copies ran while one was open for 1% of the time, Pallas kernels for 0%

commit v1 on v0

v1 whole, which is shorter than its diff:
```python
import jax
import jax.numpy as jnp
from jax import lax
from jax.experimental import pallas as pl
from jax.experimental.pallas import tpu as pltpu
from jax.sharding import PartitionSpec as P

STEP = 100


beta_one = 0.9
beta_two = 0.999
adam_eps = 1e-08
learn_rate = 0.001
decay_rate = 0.04
momentum = 0.994

F32 = jnp.float32
BF16 = jnp.bfloat16
MESH = pl.DeviceIdType.MESH

D = 1536
HALF = D // 2
SHARD_ROWS = 192
PIECE_HALF = 96
BLOCK = 48
TOKENS = 1280
TEACH = 512

X1, X2, ZW, CF = 0, 4, 6, 14
PAIR = CF + 14
YA = PAIR + 4
YB = YA + 8
XG = YB + 8
ZG = XG + 3
YG = ZG + 3
CG = YG + 3
N_COPIES = CG + 4


def kernel(
    student_ctx, out_grad, weight, teacher, teach_input, teach_ctx,
    ctx_grad, teacher_out, gradient,
    ctx_v, og_v, w_v, t_v, tin_v, tctx_v,
    mats, g_peer, g_own, g_recv,
    ya_s, ya_r, yb_s, yb_r, xg_s, xg_r, zg_s, zg_r, rows_v,
    cg_v, to_v,
    send_sem, recv_sem, in_sem, out_sem,
):
    replica, shard = lax.axis_index("replica"), lax.axis_index("shard")
    core, y = replica % 2, (replica // 2) % 4
    z = (replica // 8) * 2 + shard % 2
    x, parity = shard // 2, shard % 2
    other = 1 - core

    def device(dx=0, dy=0, dz=0, flip=False):
        xx, yy, zz = (x + dx) % 4, (y + dy) % 4, (z + dz) % 4
        cc = other if flip else core
        return {"replica": ((zz // 2) * 4 + yy) * 2 + cc, "shard": xx * 2 + zz % 2}

    partners = [device(flip=True)]
    for step in (1, 2, 3):
        partners += [device(dx=step), device(dy=step), device(dz=step)]
    barrier = pltpu.get_barrier_semaphore()
    for partner in partners:
        pl.semaphore_signal(barrier, inc=1, device_id=partner, device_id_type=MESH)

    loads = [
        pltpu.make_async_copy(src, dst, in_sem.at[i])
        for i, (src, dst) in enumerate(
            [(weight, w_v), (teacher, t_v), (out_grad, og_v), (student_ctx, ctx_v), (teach_ctx, tctx_v), (teach_input, tin_v)]
        )
    ]
    for load in loads:
        load.start()

    copies = {}

    def send(i, src, dst, target):
        copies[i] = pltpu.make_async_remote_copy(
            src_ref=src, dst_ref=dst, send_sem=send_sem.at[i], recv_sem=recv_sem.at[i],
            device_id=target, device_id_type=MESH,
        )
        copies[i].start()

    def arrived(*ids):
        for i in ids:
            copies[i].wait_recv()

    loads[0].wait()
    loads[1].wait()
    for r in range(0, SHARD_ROWS, BLOCK):
        rows = pl.ds(r, BLOCK)
        w = w_v[rows, :]
        mats[0, shard, rows, :] = w.astype(BF16)
        mats[1, shard, rows, :] = (momentum * t_v[rows, :] + (1.0 - momentum) * w).astype(BF16)

    pl.semaphore_wait(barrier, len(partners))

    def piece(dx, half, dparity=False):
        index = ((x + dx) % 4) * 2 + ((1 - parity) if dparity else parity)
        return mats.at[core, index, pl.ds(half * PIECE_HALF, PIECE_HALF)]

    def send_piece(i, ref, target):
        send(i, ref, ref, target)

    right, left, up, down = device(dx=1), device(dx=3), device(dz=1), device(dz=3)
    twin = device(flip=True)
    offsets = (0, 3, 1, 2)

    def send_z(j, half):
        send_piece(ZW + 2 * j + half, piece(offsets[j], half), up if half == 0 else down)

    def hand_over(slot, dx, half, dparity=False):
        send_piece(CF + slot, piece(dx, half, dparity), twin)

    send_piece(X1 + 0, piece(0, 0), right)
    send_piece(X1 + 2, piece(0, 1), left)
    send_z(0, 0)
    send_z(0, 1)

    north, south, far_y = device(dy=1), device(dy=3), (y + 2) % 4
    y_up, y_down = (y + 1) % 4, (y + 3) % 4

    loads[2].wait()
    loads[3].wait()

    def grad_chunk(k):
        columns = ctx_v[:, pl.ds(pl.multiple_of(((x + 1 + k) % 4) * 384, 128), 384)]

        def part(side):
            return lax.dot_general(
                columns, og_v[:, pl.ds(pl.multiple_of(side * HALF, 128), HALF)],
                (((0,), (0,)), ((), ())), preferred_element_type=F32,
            )

        g_peer[k] = part(other)
        send(PAIR + k, g_peer.at[k], g_recv.at[k], twin)
        g_own[k] = part(core)

    def block(k, par, yy):
        return g_own[k, pl.ds(pl.multiple_of(par * SHARD_ROWS + yy * BLOCK, 16), BLOCK), :]

    def y_first(k):
        arrived(PAIR + k)
        g_own[k] = g_own[k] + g_recv[k]
        ya_s[k, 0] = block(k, 0, far_y).astype(BF16)
        ya_s[k, 1] = block(k, 1, far_y).astype(BF16)
        send(YA + 2 * k, ya_s.at[k, 0], ya_r.at[k, 0], north)
        send(YA + 2 * k + 1, ya_s.at[k, 1], ya_r.at[k, 1], south)

    def y_second(k):
        yb_s[k, 0, 1] = block(k, 1, y_up).astype(BF16)
        yb_s[k, 1, 0] = block(k, 0, y_down).astype(BF16)
        arrived(YA + 2 * k, YA + 2 * k + 1)
        yb_s[k, 0, 0] = (block(k, 0, y_up) + ya_r[k, 0].astype(F32)).astype(BF16)
        yb_s[k, 1, 1] = (block(k, 1, y_down) + ya_r[k, 1].astype(F32)).astype(BF16)
        send(YB + 2 * k, yb_s.at[k, 0], yb_r.at[k, 0], north)
        send(YB + 2 * k + 1, yb_s.at[k, 1], yb_r.at[k, 1], south)

    def y_sum(k, par):
        return block(k, par, y) + yb_r[k, 0, par].astype(F32) + yb_r[k, 1, par].astype(F32)

    def y_third(k):
        arrived(YB + 2 * k, YB + 2 * k + 1)
        for par in (0, 1):
            xg_s[k, par] = y_sum(k, par).astype(BF16)
        send(XG + k, xg_s.at[k], xg_r.at[k], device(dx=1 + k))

    stores = []

    def store(src, dst):
        copy = pltpu.make_async_copy(src, dst, out_sem.at[len(stores)])
        copy.start()
        stores.append(copy)

    def ctx_columns(slot, dx):
        pair = (x + dx) % 4
        rows = mats[0, pl.ds(pair * 2, 2)].reshape(2 * SHARD_ROWS, D)

        def step(m, _):
            tokens = pl.ds(pl.multiple_of(m * 640, 128), 640)
            cg_v[slot, tokens, :] = lax.dot_general(
                og_v[tokens, :], rows, (((1,), (1,)), ((), ())), preferred_element_type=F32
            ).astype(BF16)
            return 0

        lax.fori_loop(0, TOKENS // 640, step, 0)
        store(cg_v.at[slot], ctx_grad.at[:, pl.ds(pl.multiple_of(pair * 384, 128), 384)])

    grad_chunk(0)
    grad_chunk(1)
    y_first(0)
    grad_chunk(2)
    y_first(1)
    y_second(0)
    grad_chunk(3)
    y_first(2)
    y_second(1)
    arrived(X1 + 0, X1 + 2)
    send_piece(X1 + 1, piece(0, 1), right)
    send_piece(X1 + 3, piece(0, 0), left)
    send_piece(X2 + 0, piece(3, 0), right)
    send_piece(X2 + 1, piece(1, 1), left)
    send_z(1, 0)
    send_z(2, 1)
    hand_over(0, 3, 0)
    hand_over(1, 1, 1)
    y_first(3)
    y_second(2)
    arrived(ZW + 0, ZW + 1)
    hand_over(2, 0, 0, True)
    hand_over(3, 0, 1, True)
    y_second(3)
    y_third(0)
    arrived(X1 + 1, X1 + 3)
    send_z(1, 1)
    send_z(2, 0)
    hand_over(4, 3, 1)
    hand_over(5, 1, 0)
    arrived(CF + 2, CF + 3)
    ctx_columns(0, 0)
    arrived(ZW + 2, ZW + 5)
    hand_over(6, 3, 0, True)
    hand_over(7, 1, 1, True)
    y_third(1)
    arrived(X2 + 0, X2 + 1)
    send_z(3, 0)
    send_z(3, 1)
    hand_over(8, 2, 0)
    hand_over(9, 2, 1)
    y_third(2)
    arrived(ZW + 3, ZW + 4)
    hand_over(10, 3, 1, True)
    hand_over(11, 1, 0, True)
    arrived(CF + 0, CF + 5, CF + 4, CF + 1, CF + 6, CF + 7, CF + 10, CF + 11)
    arrived(YB + 6, YB + 7, XG + 0, XG + 1, XG + 2)
    for par in (0, 1):
        total = y_sum(3, par)
        for k in range(3):
            total = total + xg_r[k, par].astype(F32)
        zg_s[par] = total
    send(ZG + 0, zg_s.at[1 - parity], zg_r.at[z], up)
    send(ZG + 1, zg_s.at[1 - parity], zg_r.at[z], down)
    send(ZG + 2, zg_s.at[parity], zg_r.at[z], device(dz=2))
    zg_r[z] = zg_s[parity]
    ctx_columns(1, 3)
    ctx_columns(2, 1)
    arrived(ZW + 6, ZW + 7)
    hand_over(12, 2, 0, True)
    hand_over(13, 2, 1, True)
    arrived(ZG + 0, ZG + 1, ZG + 2)
    rows_v[y, core] = (zg_r[0] + zg_r[1] + zg_r[2] + zg_r[3]).astype(BF16)
    own = rows_v.at[y, core]
    send(YG + 0, own, own, north)
    send(YG + 1, own, own, south)
    send(YG + 2, own, own, device(dy=2))
    send(CG + 0, own, own, twin)
    arrived(CF + 8, CF + 9, CF + 12, CF + 13)
    ctx_columns(3, 2)
    for j, source in enumerate((y_down, y_up, far_y)):
        arrived(YG + j)
        got = rows_v.at[source, core]
        send(CG + 1 + j, got, got, twin)
    loads[4].wait()
    loads[5].wait()

    def teach(n, _):
        columns = pl.ds(pl.multiple_of(n * 768, 128), 768)
        projected = jnp.dot(tctx_v[...], mats[1, :, :, columns].reshape(D, 768), preferred_element_type=F32)
        to_v[:, columns] = (tin_v[:, columns].astype(F32) + projected).astype(BF16)
        return 0

    lax.fori_loop(0, 2, teach, 0)
    store(to_v, teacher_out)
    arrived(CG + 0, CG + 1, CG + 2, CG + 3)
    for yy in range(4):
        for cc in range(2):
            store(rows_v.at[yy, cc], gradient.at[pl.ds(yy * BLOCK, BLOCK), pl.ds(cc * HALF, HALF)])
    for i in range(N_COPIES):
        copies[i].wait_send()
    for copy in stores:
        copy.wait()


def communicate(student_ctx, out_grad, weight, teacher, teach_input, teach_ctx):
    anywhere = pl.BlockSpec(memory_space=pl.ANY)
    vmem = pltpu.VMEM
    return pl.pallas_call(
        kernel,
        out_shape=(
            jax.ShapeDtypeStruct((TOKENS, D), BF16),
            jax.ShapeDtypeStruct((TEACH, D), BF16),
            jax.ShapeDtypeStruct((SHARD_ROWS, D), BF16),
        ),
        in_specs=[anywhere] * 6,
        out_specs=(anywhere,) * 3,
        scratch_shapes=[
            vmem((TOKENS, D), BF16),
            vmem((TOKENS, D), BF16),
            vmem((SHARD_ROWS, D), F32),
            vmem((SHARD_ROWS, D), F32),
            vmem((TEACH, D), BF16),
            vmem((TEACH, D), BF16),
            vmem((2, 8, SHARD_ROWS, D), BF16),
            vmem((4, 384, HALF), F32),
            vmem((4, 384, HALF), F32),
            vmem((4, 384, HALF), F32),
            vmem((4, 2, BLOCK, HALF), BF16),
            vmem((4, 2, BLOCK, HALF), BF16),
            vmem((4, 2, 2, BLOCK, HALF), BF16),
            vmem((4, 2, 2, BLOCK, HALF), BF16),
            vmem((3, 2, BLOCK, HALF), BF16),
            vmem((3, 2, BLOCK, HALF), BF16),
            vmem((2, BLOCK, HALF), F32),
            vmem((4, BLOCK, HALF), F32),
            vmem((4, 2, BLOCK, HALF), BF16),
            vmem((4, TOKENS, 384), BF16),
            vmem((TEACH, D), BF16),
            pltpu.SemaphoreType.DMA((N_COPIES,)),
            pltpu.SemaphoreType.DMA((N_COPIES,)),
            pltpu.SemaphoreType.DMA((6,)),
            pltpu.SemaphoreType.DMA((13,)),
        ],
        compiler_params=pltpu.CompilerParams(
            collective_id=0, has_side_effects=True, vmem_limit_bytes=62 * 2**20
        ),
        cost_estimate=pl.CostEstimate(
            flops=2 * D * D * (2 * TOKENS + TEACH), bytes_accessed=22 * 2**20, transcendentals=0
        ),
        name="exchange",
    )(student_ctx, out_grad, weight, teacher, teach_input, teach_ctx)


def body(student_ctx, out_grad, weight, moment_one, moment_two, teacher, teach_input, teach_ctx):
    ctx_grad, teacher_out, own_rows = communicate(
        student_ctx, out_grad, weight, teacher, teach_input, teach_ctx
    )
    teacher_next = momentum * teacher + (1.0 - momentum) * weight
    gradient = own_rows.astype(F32)
    moment_one_next = beta_one * moment_one + (1.0 - beta_one) * gradient
    moment_two_next = beta_two * moment_two + (1.0 - beta_two) * gradient * gradient
    correct_one = 1.0 - beta_one**STEP
    correct_two = 1.0 - beta_two**STEP
    update = (
        moment_one_next / correct_one / (jnp.sqrt(moment_two_next / correct_two) + adam_eps)
        + decay_rate * weight
    )
    weight_next = weight - learn_rate * update
    return (ctx_grad, weight_next, moment_one_next, moment_two_next, teacher_next, teacher_out)


def solution(mesh):
    return jax.shard_map(
        body,
        mesh=mesh,
        in_specs=(
            P(("replica", "shard"), None),
            P(("replica", "shard"), None),
            P("shard", None),
            P("shard", None),
            P("shard", None),
            P("shard", None),
            P(("replica", "shard"), None),
            P(("replica", "shard"), None),
        ),
        out_specs=(
            P(("replica", "shard"), None),
            P("shard", None),
            P("shard", None),
            P("shard", None),
            P("shard", None),
            P(("replica", "shard"), None),
        ),
        check_vma=False,
    )
```

time: 786 us -> 70.1 us (0.09)
  blocking collectives: 401 us -> 0 us
  waiting for transfers between devices: 189 us -> 0 us
  starting transfers between devices: 86.3 us -> 0 us
  Pallas kernels: 0 us -> 59.5 us
  local copies, waits for them, and re-layouts: 57.3 us -> 3.67 us
  matrix products: 28.3 us -> 0 us
  between operations: 14.9 us -> 0.67 us
    unnamed x1 -> x0, blocking collectives: 377 us -> none
    all_gather x2 -> x0, waiting for transfers between devices: 188 us -> none  [the longest x1 94.7 us: body(): lax.all_gather(teacher_half, 'shard', axis=0, tiled=True)]
    unnamed x32 -> x0, starting transfers between devices: 86.1 us -> none
    pallas_call x0 -> x1, Pallas kernels: none -> 59.5 us  [communicate(): pl.pallas_call(kernel, out_shape=(jax.ShapeDtypeStruct((TOKENS, D), BF16)...]
    unnamed x60 -> x8, local copies, waits for them, and re-layouts: 37.8 us -> 3.67 us
    dot_general x3 -> x0, matrix products: 28.3 us -> none  [the longest x1 11.5 us: body(): lax.dot_general(columns, out_grad, (((0,), (0,)), ((), ())), preferred_el...]
    all_gather x1 -> x0, blocking collectives: 23.2 us -> none  [body(): lax.all_gather(own_block.astype(jnp.bfloat16), 'replica', axis=0, tiled=T...]
    reshape x2 -> x0, local copies, waits for them, and re-layouts: 13.9 us -> none  [the longest x1 7 us: body(): virtual_ctx.transpose(0, 2, 1, 3).reshape(token_count, features)]
  transfers between devices with their start and end apart: 34 -> 0, of which waited for: 2 -> 0; matrix products, arithmetic and copies ran while one was open for 1% -> 0% of each run, Pallas kernels for 0% -> 0%
where the time goes in v1:
time: 70.1 us; the launch traced here: 69 us
  Pallas kernels  59.5 us (85%)
  other arithmetic  5.21 us (7%)
  local copies, waits for them, and re-layouts  3.67 us (5%)
    pallas_call x1, Pallas kernels, communicate(): pl.pallas_call(kernel, out_shape=(jax.ShapeDtypeStruct((TOKENS, D), BF16)...  59.5 us
    sub x1, other arithmetic, body(): weight_next = weight - learn_rate * update  5.21 us
    unnamed x8, local copies, waits for them, and re-layouts  3.67 us

profile of v1, /device:TPU:0, one launch (start us, length us, event | category | flops | bytes accessed | tf_op | source)
XLA Modules:
  0.0 69.0 jit_solution(5457052655217438989)
XLA Ops:
  0.6 0.0 copy-start.2
  0.6 59.5 %exchange.1 = (bf16[1280,1536]{1,0:T(8,128)(2,1)}, bf16[512,1536]{1,0:T(8,128)(2,1)}, bf16[192,1536]{1,0:T(8,128)(2,1)}) custom-call(bf16[1280,1536]{1,0:T(8,128)(2,1)} %student_ctx.1, bf16[1280,1536]{1,0:T(8,128)(2,1)} %out_grad.1, f32[192,1536]{1,0:T(8,128)} %weight.1, f32[192,1536]{1,0:T(8,128)} %teacher.1, bf16[512,1536]{1,0:T(8,128)(2,1)} %teach_input.1, ...), custom_call_target="tpu_custom_call" | custom-call | flops 14495514624 | bytes 23068672 | tf_op jit(solution)/shard_map/exchange/pallas_call | solution.py:289
  60.1 0.0 copy-done.2
  60.1 0.0 copy-start
  60.1 5.2 %multiply_subtract_fusion = (f32[192,1536]{1,0:T(8,128)}, f32[192,1536]{1,0:T(8,128)}, f32[192,1536]{1,0:T(8,128)}, f32[192,1536]{1,0:T(8,128)}) fusion(f32[192,1536]{1,0:T(8,128)S(1)} %copy-done.2, bf16[192,1536]{1,0:T(8,128)(2,1)} %get-tuple-element.10, f32[192,1536]{1,0:T(8,128)} %param.11, f32[192,1536]{1,0:T(8,128)} %param.12, f32[192,1536]{1,0:T(8,128)} %teacher.1), kind=kLoop, calls=%fused_computation.5 | loop fusion | flops 5603328 | bytes 10027008 | tf_op jit(solution)/shard_map/sub | solution.py:349
  65.3 0.0 copy-done
  65.3 0.0 copy-start.1
  65.3 1.9 %copy.16 = bf16[1280,1536]{1,0:T(8,128)(2,1)} copy(bf16[1280,1536]{1,0:T(8,128)(2,1)S(1)} %copy-done) | data formatting | bytes 7864320
  67.3 0.6 copy-done.1
  67.9 1.1 %copy.17 = bf16[512,1536]{1,0:T(8,128)(2,1)} copy(bf16[512,1536]{1,0:T(8,128)(2,1)S(1)} %copy-done.1) | data formatting | bytes 3145728
Async XLA Ops:
  0.6 59.5 %copy-start.2 = (f32[192,1536]{1,0:T(8,128)S(1)}, f32[192,1536]{1,0:T(8,128)}, u32[]{:S(2)}) copy-start(f32[192,1536]{1,0:T(8,128)} %weight.1) | copy-start | bytes 3538948
  60.1 5.2 %copy-start = (bf16[1280,1536]{1,0:T(8,128)(2,1)S(1)}, bf16[1280,1536]{1,0:T(8,128)(2,1)}, u32[]{:S(2)}) copy-start(bf16[1280,1536]{1,0:T(8,128)(2,1)} %get-tuple-element.22) | copy-start | bytes 11796484
  65.3 2.5 %copy-start.1 = (bf16[512,1536]{1,0:T(8,128)(2,1)S(1)}, bf16[512,1536]{1,0:T(8,128)(2,1)}, u32[]{:S(2)}) copy-start(bf16[512,1536]{1,0:T(8,128)(2,1)} %get-tuple-element.27) | copy-start | bytes 4718596

commit v2 on v0

v2 whole, which is shorter than its diff:
```python
import jax
import jax.numpy as jnp
from jax import lax
from jax.experimental import pallas as pl
from jax.experimental.pallas import tpu as pltpu
from jax.sharding import PartitionSpec as P

STEP = 100


beta_one = 0.9
beta_two = 0.999
adam_eps = 1e-08
learn_rate = 0.001
decay_rate = 0.04
momentum = 0.994

F32 = jnp.float32
BF16 = jnp.bfloat16
MESH = pl.DeviceIdType.MESH

D = 1536
HALF = D // 2
SHARD_ROWS = 192
PIECE_HALF = 96
BLOCK = 48
TOKENS = 1280
TEACH = 512

THIRD = 256
ORDER = (2, 1, 3, 0)
LANES = 128

sizes = dict(
    X1=6, X2=2, ZW=8, YW=10, CF=14, PAIR=4,
    Y1=12, Z1=12, XA=3, XB=3, ZB=3, YB=3, ZC=3, YC=3, XC=3, GA=7, GC=8,
)
first = {}
N_COPIES = 0
for name, size in sizes.items():
    first[name] = N_COPIES
    N_COPIES += size


def kernel(
    student_ctx, out_grad, weight, teacher, teach_input, teach_ctx,
    ctx_grad, teacher_out, gradient,
    ctx_v, og_v, w_v, t_v, tin_v, tctx_v,
    mats, g_peer, g_own, g_recv,
    y1_s, y1_r, z1_s, z1_r, xa_s, xa_r,
    xb_s, xb_r, zb_s, zb_r, yb_s, yb_r,
    zc_s, zc_r, yc_s, yc_r, xc_s, xc_r,
    rows_v, sum_v,
    send_sem, recv_sem, in_sem,
):
    replica, shard = lax.axis_index("replica"), lax.axis_index("shard")
    core, y = replica % 2, (replica // 2) % 4
    z_high = replica // 8
    z = z_high * 2 + shard % 2
    x, parity = shard // 2, shard % 2
    other = 1 - core
    h = y % 2

    def device(dx=0, dy=0, dz=0, flip=False):
        xx, yy, zz = (x + dx) % 4, (y + dy) % 4, (z + dz) % 4
        cc = other if flip else core
        return {"replica": ((zz // 2) * 4 + yy) * 2 + cc, "shard": xx * 2 + zz % 2}

    partners = [device(flip=True)]
    for step in (1, 2, 3):
        partners += [device(dx=step), device(dy=step), device(dz=step), device(dy=step, dz=2)]
    barrier = pltpu.get_barrier_semaphore()
    for partner in partners:
        pl.semaphore_signal(barrier, inc=1, device_id=partner, device_id_type=MESH)

    def ctx_columns_at(k):
        return pl.ds(pl.multiple_of(((x + ORDER[k]) % 4) * 384, 128), 384)

    pairs = [(weight, w_v), (teacher, t_v), (out_grad, og_v)]
    pairs += [(student_ctx.at[:, ctx_columns_at(k)], ctx_v.at[k]) for k in range(4)]
    pairs += [(teach_ctx, tctx_v), (teach_input, tin_v)]
    loads = [pltpu.make_async_copy(src, dst, in_sem.at[i]) for i, (src, dst) in enumerate(pairs)]
    for i in range(4):
        loads[i].start()

    copies = {}

    def send(name, i, src, dst, target):
        copies[name, i] = pltpu.make_async_remote_copy(
            src_ref=src, dst_ref=dst,
            send_sem=send_sem.at[first[name] + i], recv_sem=recv_sem.at[first[name] + i],
            device_id=target, device_id_type=MESH,
        )
        copies[name, i].start()

    def arrived(name, *ids):
        for i in ids:
            copies[name, i].wait_recv()

    loads[0].wait()
    loads[1].wait()
    for r in range(0, SHARD_ROWS, BLOCK):
        rows = pl.ds(r, BLOCK)
        w = w_v[rows, :]
        mats[0, shard, rows, :] = w.astype(BF16)
        mats[1, shard, rows, :] = (momentum * t_v[rows, :] + (1.0 - momentum) * w).astype(BF16)

    for i in range(4, 9):
        loads[i].start()
    pl.semaphore_wait(barrier, len(partners))

    right, left, up, down = device(dx=1), device(dx=3), device(dz=1), device(dz=3)
    north, south, twin = device(dy=1), device(dy=3), device(flip=True)
    offsets = (0, 3, 1, 2)

    def piece(dx, start, size, flipped):
        index = ((x + dx) % 4) * 2 + ((1 - parity) if flipped else parity)
        return mats.at[core, index, pl.ds(pl.multiple_of(start, 16), size)]

    def half(dx, near, flipped=False):
        return piece(dx, (h if near else 1 - h) * 96, 96, flipped)

    def quarter(dx, q, flipped=False):
        return piece(dx, h * 96 + q * 48, 48, flipped)

    def pass_on(name, i, ref, target):
        send(name, i, ref, ref, target)

    def send_z(j, q):
        pass_on("ZW", 2 * j + q, quarter(offsets[j], q), up if q == 0 else down)

    def send_y(j, q):
        ref = quarter(offsets[j], q, True) if j < 4 else quarter(2, q)
        pass_on("YW", 2 * j + q, ref, north if q == 0 else south)

    def hand_over(slot, ref):
        pass_on("CF", slot, ref, twin)

    def z_event(j):
        arrived("ZW", 2 * j, 2 * j + 1)
        send_y(j, 0)
        send_y(j, 1)
        hand_over(6 + 2 * j, half(offsets[j], True, True))

    def y_event(j):
        arrived("YW", 2 * j, 2 * j + 1)
        if j < 4:
            hand_over(7 + 2 * j, half(offsets[j], False, True))
        else:
            hand_over(5, half(2, False))

    pass_on("X1", 0, quarter(0, 0), right)
    pass_on("X1", 1, quarter(0, 1), left)
    pass_on("X1", 2, quarter(0, 1), right)
    pass_on("X1", 3, quarter(0, 0), left)
    send_z(0, 0)
    send_z(0, 1)

    def grad_part(k, side):
        return lax.dot_general(
            ctx_v[k], og_v[:, pl.ds(pl.multiple_of(side * HALF, 128), HALF)],
            (((0,), (0,)), ((), ())), preferred_element_type=F32,
        )

    def grad_peer(k):
        loads[3 + k].wait()
        g_peer[k] = grad_part(k, other)
        send("PAIR", k, g_peer.at[k], g_recv.at[k], twin)

    def grad_own(k):
        g_own[k] = grad_part(k, core)

    def both(k, row, n_rows, column, n_columns):
        at = (k, pl.ds(pl.multiple_of(row, 16), n_rows), pl.ds(pl.multiple_of(column, 128), n_columns))
        return g_own[at] + g_recv[at]

    def phase_one(k):
        arrived("PAIR", k)
        if k < 3:
            xa_s[k] = both(k, 0, 384, THIRD, THIRD).astype(BF16)
            send("XA", k, xa_s.at[k], xa_r.at[k], device(dx=ORDER[k]))
        for j in range(3):
            yy = (y + 1 + j) % 4
            for par in (0, 1):
                y1_s[k, j, par] = both(k, par * SHARD_ROWS + yy * BLOCK, BLOCK, 0, THIRD).astype(BF16)
            send("Y1", 3 * k + j, y1_s.at[k, j], y1_r.at[k, j], device(dy=1 + j))
            zz = (z + 1 + j) % 4
            z1_s[k, j] = both(
                k, (zz % 2) * SHARD_ROWS, SHARD_ROWS, 2 * THIRD + (zz // 2) * LANES, LANES
            ).astype(BF16)
            send("Z1", 3 * k + j, z1_s.at[k, j], z1_r.at[k, j], device(dz=1 + j))

    def first_y(k):
        arrived("Y1", 3 * k, 3 * k + 1, 3 * k + 2)
        for par in (0, 1):
            total = both(k, par * SHARD_ROWS + y * BLOCK, BLOCK, 0, THIRD)
            for j in range(3):
                total = total + y1_r[k, j, par].astype(F32)
            xb_s[k, par] = total
        if k < 3:
            send("XB", k, xb_s.at[k], xb_r.at[k], device(dx=ORDER[k]))

    def first_z(k):
        arrived("Z1", 3 * k, 3 * k + 1, 3 * k + 2)
        for yy in range(4):
            rows = pl.ds(yy * BLOCK, BLOCK)
            total = both(k, parity * SHARD_ROWS + yy * BLOCK, BLOCK, 2 * THIRD + z_high * LANES, LANES)
            for j in range(3):
                total = total + z1_r[k, j, rows, :].astype(F32)
            yb_s[yy, k] = total

    def first_x():
        arrived("XA", 0, 1, 2)
        for par in (0, 1):
            for zh in (0, 1):
                for q in range(4):
                    rows = pl.ds(par * SHARD_ROWS + q * BLOCK, BLOCK)
                    lanes = pl.ds(zh * LANES, LANES)
                    total = both(3, par * SHARD_ROWS + q * BLOCK, BLOCK, THIRD + zh * LANES, LANES)
                    for k in range(3):
                        total = total + xa_r[k, rows, lanes].astype(F32)
                    zb_s[par, zh, q * BLOCK:(q + 1) * BLOCK, :] = total
        for j in range(3):
            zz = (z + 1 + j) % 4
            send("ZB", j, zb_s.at[zz % 2, zz // 2], zb_r.at[j], device(dz=1 + j))

    def second_y():
        for j in range(3):
            send("YB", j, yb_s.at[(y + 1 + j) % 4], yb_r.at[j], device(dy=1 + j))

    def third_z():
        arrived("XB", 0, 1, 2)
        for par in (0, 1):
            for zh in (0, 1):
                lanes = pl.ds(zh * LANES, LANES)
                zc_s[par, zh] = (
                    xb_s[3, par, :, lanes] + xb_r[0, par, :, lanes] + xb_r[1, par, :, lanes] + xb_r[2, par, :, lanes]
                )
        for j in range(3):
            zz = (z + 1 + j) % 4
            send("ZC", j, zc_s.at[zz % 2, zz // 2], zc_r.at[j], device(dz=1 + j))

    def third_y():
        arrived("ZB", 0, 1, 2)
        for yy in range(4):
            rows = pl.ds(yy * BLOCK, BLOCK)
            yc_s[yy] = zb_s[parity, z_high, rows, :] + zb_r[0, rows, :] + zb_r[1, rows, :] + zb_r[2, rows, :]
        for j in range(3):
            send("YC", j, yc_s.at[(y + 1 + j) % 4], yc_r.at[j], device(dy=1 + j))

    def third_x():
        arrived("YB", 0, 1, 2)
        for k in range(4):
            xc_s[k] = yb_s[y, k] + yb_r[0, k] + yb_r[1, k] + yb_r[2, k]
        for k in range(3):
            send("XC", k, xc_s.at[k], xc_r.at[k], device(dx=ORDER[k]))

    steps = [(0, 1), (0, 3), (0, 2), (2, 0), (2, 1), (2, 3), (2, 2)]

    def share():
        arrived("ZC", 0, 1, 2)
        rows_v[z_high, y, core, 0] = (
            zc_s[parity, z_high] + zc_r[0] + zc_r[1] + zc_r[2]
        ).astype(BF16)
        arrived("YC", 0, 1, 2)
        rows_v[z_high, y, core, 1] = (yc_s[y] + yc_r[0] + yc_r[1] + yc_r[2]).astype(BF16)
        arrived("XC", 0, 1, 2)
        rows_v[z_high, y, core, 2] = (xc_s[3] + xc_r[0] + xc_r[1] + xc_r[2]).astype(BF16)
        own = rows_v.at[z_high, y, core]
        for i, (dz, dy) in enumerate(steps):
            send("GA", i, own, own, device(dy=dy, dz=dz))
        send("GC", 7, own, own, twin)

    def share_on():
        for i, (dz, dy) in enumerate(steps):
            arrived("GA", i)
            got = rows_v.at[(z_high + dz // 2) % 2, (y + 4 - dy) % 4, core]
            send("GC", i, got, got, twin)

    def place(zh, yy):
        for cc in range(2):
            for third in range(3):
                start = cc * HALF + third * THIRD + zh * LANES
                gradient[yy * BLOCK:(yy + 1) * BLOCK, start:start + LANES] = rows_v[zh, yy, cc, third]

    def columns_of(dx):
        return pl.ds(pl.multiple_of(((x + dx) % 4) * 384, 128), 384)

    def pieces_of(m, dx):
        return mats[m, pl.ds(((x + dx) % 4) * 2, 2)].reshape(2 * SHARD_ROWS, D)

    def ctx_work(dx):
        ctx_grad[:, columns_of(dx)] = lax.dot_general(
            og_v[...], pieces_of(0, dx), (((1,), (1,)), ((), ())), preferred_element_type=F32
        ).astype(BF16)

    def teach_part(dx, at):
        return jnp.dot(
            tctx_v[:, columns_of(dx)], mats[1, pl.ds(((x + dx) % 4) * 2, 2), :, at].reshape(2 * SHARD_ROWS, HALF),
            preferred_element_type=F32,
        )

    def teach_most():
        def step(n, _):
            at = pl.ds(pl.multiple_of(n * HALF, 128), HALF)
            sum_v[:, at] = teach_part(0, at) + teach_part(3, at) + teach_part(1, at)
            return 0

        lax.fori_loop(0, 2, step, 0)

    def teach_rest():
        def step(n, _):
            at = pl.ds(pl.multiple_of(n * HALF, 128), HALF)
            teacher_out[:, at] = (tin_v[:, at].astype(F32) + (sum_v[:, at] + teach_part(2, at))).astype(BF16)
            return 0

        lax.fori_loop(0, 2, step, 0)

    def x_event_first():
        arrived("X1", 0, 1)
        pass_on("X2", 0, quarter(3, 0), right)
        pass_on("X2", 1, quarter(1, 1), left)
        send_z(1, 0)
        send_z(2, 1)

    def x_event_second():
        arrived("X1", 2, 3)
        send_z(1, 1)
        send_z(2, 0)
        hand_over(0, half(3, True))
        hand_over(1, half(1, True))

    def opposite_event():
        arrived("X2", 0, 1)
        send_z(3, 0)
        send_z(3, 1)
        send_y(4, 0)
        send_y(4, 1)
        hand_over(4, half(2, True))

    loads[2].wait()
    grad_peer(0)
    grad_peer(1)
    grad_own(0)
    phase_one(0)
    grad_peer(2)
    grad_own(1)
    x_event_first()
    phase_one(1)
    grad_peer(3)
    grad_own(2)
    z_event(0)
    phase_one(2)
    grad_own(3)
    x_event_second()
    opposite_event()
    phase_one(3)
    pass_on("X1", 4, half(0, False), right)
    pass_on("X1", 5, half(0, False), left)
    first_y(0)
    first_z(0)
    first_y(1)
    first_z(1)
    y_event(0)
    first_y(2)
    first_z(2)
    z_event(1)
    z_event(2)
    first_x()
    first_y(3)
    first_z(3)
    second_y()
    z_event(3)
    loads[7].wait()
    loads[8].wait()
    arrived("CF", 6, 7)
    ctx_work(0)
    y_event(4)
    third_z()
    third_y()
    third_x()
    y_event(1)
    y_event(2)
    arrived("X1", 4, 5)
    hand_over(2, half(3, False))
    hand_over(3, half(1, False))
    y_event(3)
    share()
    arrived("CF", 0, 2, 8, 9, 1, 3, 10, 11)
    ctx_work(3)
    ctx_work(1)
    teach_most()
    share_on()
    arrived("CF", 4, 5, 12, 13)
    ctx_work(2)
    teach_rest()
    arrived("GC", *range(8))
    for zh in range(2):
        for yy in range(4):
            place(zh, yy)
    for copy in copies.values():
        copy.wait_send()


def communicate(student_ctx, out_grad, weight, teacher, teach_input, teach_ctx):
    anywhere = pl.BlockSpec(memory_space=pl.ANY)
    vmem = pltpu.VMEM
    return pl.pallas_call(
        kernel,
        out_shape=(
            pltpu.VMEM((TOKENS, D), BF16),
            pltpu.VMEM((TEACH, D), BF16),
            pltpu.VMEM((SHARD_ROWS, D), BF16),
        ),
        in_specs=[anywhere] * 6,
        out_specs=(pl.BlockSpec(memory_space=pltpu.VMEM),) * 3,
        scratch_shapes=[
            vmem((4, TOKENS, 384), BF16),
            vmem((TOKENS, D), BF16),
            vmem((SHARD_ROWS, D), F32),
            vmem((SHARD_ROWS, D), F32),
            vmem((TEACH, D), BF16),
            vmem((TEACH, D), BF16),
            vmem((2, 8, SHARD_ROWS, D), BF16),
            vmem((4, 384, HALF), F32),
            vmem((4, 384, HALF), F32),
            vmem((4, 384, HALF), F32),
            vmem((4, 3, 2, BLOCK, THIRD), BF16),
            vmem((4, 3, 2, BLOCK, THIRD), BF16),
            vmem((4, 3, SHARD_ROWS, LANES), BF16),
            vmem((4, 3, SHARD_ROWS, LANES), BF16),
            vmem((3, 384, THIRD), BF16),
            vmem((3, 384, THIRD), BF16),
            vmem((4, 2, BLOCK, THIRD), F32),
            vmem((3, 2, BLOCK, THIRD), F32),
            vmem((2, 2, SHARD_ROWS, LANES), F32),
            vmem((3, SHARD_ROWS, LANES), F32),
            vmem((4, 4, BLOCK, LANES), F32),
            vmem((3, 4, BLOCK, LANES), F32),
            vmem((2, 2, BLOCK, LANES), F32),
            vmem((3, BLOCK, LANES), F32),
            vmem((4, BLOCK, LANES), F32),
            vmem((3, BLOCK, LANES), F32),
            vmem((4, BLOCK, LANES), F32),
            vmem((3, BLOCK, LANES), F32),
            vmem((2, 4, 2, 3, BLOCK, LANES), BF16),
            vmem((TEACH, D), F32),
            pltpu.SemaphoreType.DMA((N_COPIES,)),
            pltpu.SemaphoreType.DMA((N_COPIES,)),
            pltpu.SemaphoreType.DMA((9,)),
        ],
        compiler_params=pltpu.CompilerParams(
            collective_id=0, has_side_effects=True, vmem_limit_bytes=54 * 2**20
        ),
        cost_estimate=pl.CostEstimate(
            flops=2 * D * D * (2 * TOKENS + TEACH), bytes_accessed=22 * 2**20, transcendentals=0
        ),
        name="exchange",
    )(student_ctx, out_grad, weight, teacher, teach_input, teach_ctx)


def finish_kernel(
    ctx_grad, teacher_out, gradient, weight, moment_one, moment_two, teacher,
    ctx_grad_o, weight_o, moment_one_o, moment_two_o, teacher_o, teacher_out_o,
    w_v, one_v, two_v, t_v, wo_v, oneo_v, twoo_v, to_v, in_sem, out_sem,
):
    loads = [
        pltpu.make_async_copy(src, dst, in_sem.at[i])
        for i, (src, dst) in enumerate([(weight, w_v), (moment_one, one_v), (moment_two, two_v), (teacher, t_v)])
    ]
    for load in loads:
        load.start()
    stores = []

    def store(src, dst):
        copy = pltpu.make_async_copy(src, dst, out_sem.at[len(stores)])
        copy.start()
        stores.append(copy)

    for r in range(4):
        rows = pl.ds(r * (TOKENS // 4), TOKENS // 4)
        store(ctx_grad.at[rows], ctx_grad_o.at[rows])
    for r in range(2):
        rows = pl.ds(r * (TEACH // 2), TEACH // 2)
        store(teacher_out.at[rows], teacher_out_o.at[rows])
    for load in loads:
        load.wait()
    correct_one = 1.0 - beta_one**STEP
    correct_two = 1.0 - beta_two**STEP
    for r in range(4):
        rows = pl.ds(r * BLOCK, BLOCK)
        g, w = gradient[rows, :].astype(F32), w_v[rows, :]
        one = beta_one * one_v[rows, :] + (1.0 - beta_one) * g
        two = beta_two * two_v[rows, :] + (1.0 - beta_two) * g * g
        update = one / correct_one / (jnp.sqrt(two / correct_two) + adam_eps) + decay_rate * w
        wo_v[rows, :] = w - learn_rate * update
        oneo_v[rows, :] = one
        twoo_v[rows, :] = two
        to_v[rows, :] = momentum * t_v[rows, :] + (1.0 - momentum) * w
        for src, dst in ((wo_v, weight_o), (oneo_v, moment_one_o), (twoo_v, moment_two_o), (to_v, teacher_o)):
            store(src.at[rows], dst.at[rows])
    for copy in stores:
        copy.wait()


def finish(ctx_grad, teacher_out, gradient, weight, moment_one, moment_two, teacher):
    anywhere, near = pl.BlockSpec(memory_space=pl.ANY), pl.BlockSpec(memory_space=pltpu.VMEM)
    state = jax.ShapeDtypeStruct((SHARD_ROWS, D), F32)
    return pl.pallas_call(
        finish_kernel,
        out_shape=(
            jax.ShapeDtypeStruct((TOKENS, D), BF16), state, state, state, state,
            jax.ShapeDtypeStruct((TEACH, D), BF16),
        ),
        in_specs=[near] * 3 + [anywhere] * 4,
        out_specs=(anywhere,) * 6,
        scratch_shapes=[pltpu.VMEM((SHARD_ROWS, D), F32)] * 8
        + [pltpu.SemaphoreType.DMA((4,)), pltpu.SemaphoreType.DMA((22,))],
        compiler_params=pltpu.CompilerParams(vmem_limit_bytes=24 * 2**20),
        cost_estimate=pl.CostEstimate(flops=10 * SHARD_ROWS * D, bytes_accessed=16 * 2**20, transcendentals=0),
        name="finish",
    )(ctx_grad, teacher_out, gradient, weight, moment_one, moment_two, teacher)


def body(student_ctx, out_grad, weight, moment_one, moment_two, teacher, teach_input, teach_ctx):
    ctx_grad, teacher_out, gradient = communicate(
        student_ctx, out_grad, weight, teacher, teach_input, teach_ctx
    )
    return finish(ctx_grad, teacher_out, gradient, weight, moment_one, moment_two, teacher)


def solution(mesh):
    return jax.shard_map(
        body,
        mesh=mesh,
        in_specs=(
            P(("replica", "shard"), None),
            P(("replica", "shard"), None),
            P("shard", None),
            P("shard", None),
            P("shard", None),
            P("shard", None),
            P(("replica", "shard"), None),
            P(("replica", "shard"), None),
        ),
        out_specs=(
            P(("replica", "shard"), None),
            P("shard", None),
            P("shard", None),
            P("shard", None),
            P("shard", None),
            P(("replica", "shard"), None),
        ),
        check_vma=False,
    )
```

time: 786 us -> 66.4 us (0.08)
  blocking collectives: 401 us -> 0 us
  waiting for transfers between devices: 189 us -> 0 us
  starting transfers between devices: 86.3 us -> 0 us
  Pallas kernels: 0 us -> 63.9 us
  local copies, waits for them, and re-layouts: 57.3 us -> 1.28 us
  matrix products: 28.3 us -> 0 us
  between operations: 14.9 us -> 0.86 us
    unnamed x1 -> x0, blocking collectives: 377 us -> none
    all_gather x2 -> x0, waiting for transfers between devices: 188 us -> none  [the longest x1 94.7 us: body(): lax.all_gather(teacher_half, 'shard', axis=0, tiled=True)]
    unnamed x32 -> x0, starting transfers between devices: 86.1 us -> none
    pallas_call x0 -> x2, Pallas kernels: none -> 63.9 us  [the longest x1 58.9 us: communicate(): pl.pallas_call(kernel, out_shape=(pltpu.VMEM((TOKENS, D), BF16), pltpu.VM...]
    unnamed x60 -> x8, local copies, waits for them, and re-layouts: 37.8 us -> 1.28 us
    dot_general x3 -> x0, matrix products: 28.3 us -> none  [the longest x1 11.5 us: body(): lax.dot_general(columns, out_grad, (((0,), (0,)), ((), ())), preferred_el...]
    all_gather x1 -> x0, blocking collectives: 23.2 us -> none  [body(): lax.all_gather(own_block.astype(jnp.bfloat16), 'replica', axis=0, tiled=T...]
    reshape x2 -> x0, local copies, waits for them, and re-layouts: 13.9 us -> none  [the longest x1 7 us: body(): virtual_ctx.transpose(0, 2, 1, 3).reshape(token_count, features)]
  transfers between devices with their start and end apart: 34 -> 0, of which waited for: 2 -> 0; matrix products, arithmetic and copies ran while one was open for 1% -> 0% of each run, Pallas kernels for 0% -> 0%
where the time goes in v2:
time: 66.4 us; the launch traced here: 66 us
  Pallas kernels  63.9 us (96%)
  local copies, waits for them, and re-layouts  1.28 us (2%)
  between operations  0.86 us (1%)
    pallas_call x1, Pallas kernels, communicate(): pl.pallas_call(kernel, out_shape=(pltpu.VMEM((TOKENS, D), BF16), pltpu.VM...  58.9 us
    pallas_call x1, Pallas kernels, finish(): pl.pallas_call(finish_kernel, out_shape=(jax.ShapeDtypeStruct((TOKENS, D)...  5.01 us

profile of v2, /device:TPU:0, one launch (start us, length us, event | category | flops | bytes accessed | tf_op | source)
XLA Modules:
  0.0 66.0 jit_solution(8108840762599174945)
XLA Ops:
  0.6 0.0 copy-start.1
  0.6 0.0 copy-start
  0.7 0.0 copy-start.2
  0.7 58.9 %exchange.1 = (bf16[1280,1536]{1,0:T(8,128)(2,1)S(1)}, bf16[512,1536]{1,0:T(8,128)(2,1)S(1)}, bf16[192,1536]{1,0:T(8,128)(2,1)S(1)}) custom-call(bf16[1280,1536]{1,0:T(8,128)(2,1)} %student_ctx.1, bf16[1280,1536]{1,0:T(8,128)(2,1)} %out_grad.1, f32[192,1536]{1,0:T(8,128)} %weight.3, f32[192,1536]{1,0:T(8,128)} %teacher.3, bf16[512,1536]{1,0:T(8,128)(2,1)} %teach_input.1, ...), custom_call_target="tpu_custom_call" | custom-call | flops 14495514624 | bytes 23068672 | tf_op jit(solution)/shard_map/exchange/pallas_call | solution.py:408
  59.5 0.0 copy-done.1
  59.6 0.0 copy-done
  59.6 0.0 copy-done.2
  59.6 0.0 copy-start.3
  59.6 1.3 %copy-done.3 = f32[192,1536]{1,0:T(8,128)S(1)} copy-done((f32[192,1536]{1,0:T(8,128)S(1)}, f32[192,1536]{1,0:T(8,128)}, u32[]{:S(2)}) %copy-start.3) | copy-done | bytes 1179672
  60.8 5.0 %finish.1 = (bf16[1280,1536]{1,0:T(8,128)(2,1)}, f32[192,1536]{1,0:T(8,128)}, f32[192,1536]{1,0:T(8,128)}, f32[192,1536]{1,0:T(8,128)}, f32[192,1536]{1,0:T(8,128)}, /*index=5*/bf16[512,1536]{1,0:T(8,128)(2,1)}) custom-call(bf16[1280,1536]{1,0:T(8,128)(2,1)S(1)} %get-tuple-element.9.ctx_grad, bf16[512,1536]{1,0:T(8,128)(2,1)S(1)} %get-tuple-element.10.teacher_out, ...), custom_call_target="tpu_custom_call" | custom-call | flops 2949120 | bytes 16777216 | tf_op jit(solution)/shard_map/finish/pallas_call | solution.py:509
Async XLA Ops:
  0.6 58.9 %copy-start.1 = (f32[192,1536]{1,0:T(8,128)S(1)}, f32[192,1536]{1,0:T(8,128)}, u32[]{:S(2)}) copy-start(f32[192,1536]{1,0:T(8,128)} %teacher.3) | copy-start | bytes 3538948
  0.6 58.9 %copy-start = (f32[192,1536]{1,0:T(8,128)S(1)}, f32[192,1536]{1,0:T(8,128)}, u32[]{:S(2)}) copy-start(f32[192,1536]{1,0:T(8,128)} %weight.3) | copy-start | bytes 3538948
  0.7 58.9 %copy-start.2 = (f32[192,1536]{1,0:T(8,128)S(1)}, f32[192,1536]{1,0:T(8,128)}, u32[]{:S(2)}) copy-start(f32[192,1536]{1,0:T(8,128)} %moment_one.1) | copy-start | bytes 3538948
  59.6 1.3 %copy-start.3 = (f32[192,1536]{1,0:T(8,128)S(1)}, f32[192,1536]{1,0:T(8,128)}, u32[]{:S(2)}) copy-start(f32[192,1536]{1,0:T(8,128)} %moment_two.1) | copy-start | bytes 3538948

commit v3 on v2

--- a/solution.py
+++ b/solution.py
@@ -32,7 +32,7 @@
 LANES = 128
 
 sizes = dict(
-    X1=6, X2=2, ZW=8, YW=10, CF=14, PAIR=4,
+    X1=6, X2=2, ZW=8, YW=8, CF=14, PAIR=4,
     Y1=12, Z1=12, XA=3, XB=3, ZB=3, YB=3, ZC=3, YC=3, XC=3, GA=7, GC=8,
 )
 first = {}
@@ -43,9 +43,9 @@
 
 
 def kernel(
-    student_ctx, out_grad, weight, teacher, teach_input, teach_ctx,
-    ctx_grad, teacher_out, gradient,
-    ctx_v, og_v, w_v, t_v, tin_v, tctx_v,
+    student_ctx, out_grad, weight, moment_one, moment_two, teacher, teach_input, teach_ctx,
+    ctx_grad, teacher_out, gradient, w_v, one_v, two_v, next_v,
+    ctx_v, og_v, t_v, tin_v, tctx_v,
     mats, g_peer, g_own, g_recv,
     y1_s, y1_r, z1_s, z1_r, xa_s, xa_r,
     xb_s, xb_r, zb_s, zb_r, yb_s, yb_r,
@@ -78,7 +78,7 @@
 
     pairs = [(weight, w_v), (teacher, t_v), (out_grad, og_v)]
     pairs += [(student_ctx.at[:, ctx_columns_at(k)], ctx_v.at[k]) for k in range(4)]
-    pairs += [(teach_ctx, tctx_v), (teach_input, tin_v)]
+    pairs += [(teach_ctx, tctx_v), (teach_input, tin_v), (moment_one, one_v), (moment_two, two_v)]
     loads = [pltpu.make_async_copy(src, dst, in_sem.at[i]) for i, (src, dst) in enumerate(pairs)]
     for i in range(4):
         loads[i].start()
@@ -103,9 +103,11 @@
         rows = pl.ds(r, BLOCK)
         w = w_v[rows, :]
         mats[0, shard, rows, :] = w.astype(BF16)
-        mats[1, shard, rows, :] = (momentum * t_v[rows, :] + (1.0 - momentum) * w).astype(BF16)
-
-    for i in range(4, 9):
+        blend = momentum * t_v[rows, :] + (1.0 - momentum) * w
+        next_v[rows, :] = blend
+        mats[1, shard, rows, :] = blend.astype(BF16)
+
+    for i in range(4, 11):
         loads[i].start()
     pl.semaphore_wait(barrier, len(partners))
 
@@ -127,23 +129,27 @@
         send(name, i, ref, ref, target)
 
     def send_z(j, q):
-        pass_on("ZW", 2 * j + q, quarter(offsets[j], q), up if q == 0 else down)
+        ref = quarter(offsets[j], q) if j else piece(0, q * 96, 96, False)
+        pass_on("ZW", 2 * j + q, ref, up if q == 0 else down)
 
     def send_y(j, q):
         ref = quarter(offsets[j], q, True) if j < 4 else quarter(2, q)
-        pass_on("YW", 2 * j + q, ref, north if q == 0 else south)
+        pass_on("YW", 2 * j - 2 + q, ref, north if q == 0 else south)
 
     def hand_over(slot, ref):
         pass_on("CF", slot, ref, twin)
 
     def z_event(j):
         arrived("ZW", 2 * j, 2 * j + 1)
-        send_y(j, 0)
-        send_y(j, 1)
         hand_over(6 + 2 * j, half(offsets[j], True, True))
+        if j == 0:
+            hand_over(7, half(0, False, True))
+        else:
+            send_y(j, 0)
+            send_y(j, 1)
 
     def y_event(j):
-        arrived("YW", 2 * j, 2 * j + 1)
+        arrived("YW", 2 * j - 2, 2 * j - 1)
         if j < 4:
             hand_over(7 + 2 * j, half(offsets[j], False, True))
         else:
@@ -300,10 +306,18 @@
             preferred_element_type=F32,
         )
 
+    def teach_first():
+        def step(n, _):
+            at = pl.ds(pl.multiple_of(n * HALF, 128), HALF)
+            sum_v[:, at] = teach_part(0, at)
+            return 0
+
+        lax.fori_loop(0, 2, step, 0)
+
     def teach_most():
         def step(n, _):
             at = pl.ds(pl.multiple_of(n * HALF, 128), HALF)
-            sum_v[:, at] = teach_part(0, at) + teach_part(3, at) + teach_part(1, at)
+            sum_v[:, at] = sum_v[:, at] + (teach_part(3, at) + teach_part(1, at))
             return 0
 
         lax.fori_loop(0, 2, step, 0)
@@ -361,7 +375,6 @@
     first_z(0)
     first_y(1)
     first_z(1)
-    y_event(0)
     first_y(2)
     first_z(2)
     z_event(1)
@@ -371,10 +384,11 @@
     first_z(3)
     second_y()
     z_event(3)
-    loads[7].wait()
-    loads[8].wait()
+    for i in range(7, 11):
+        loads[i].wait()
     arrived("CF", 6, 7)
     ctx_work(0)
+    teach_first()
     y_event(4)
     third_z()
     third_y()
@@ -402,7 +416,7 @@
         copy.wait_send()
 
 
-def communicate(student_ctx, out_grad, weight, teacher, teach_input, teach_ctx):
+def communicate(*operands):
     anywhere = pl.BlockSpec(memory_space=pl.ANY)
     vmem = pltpu.VMEM
     return pl.pallas_call(
@@ -411,13 +425,13 @@
             pltpu.VMEM((TOKENS, D), BF16),
             pltpu.VMEM((TEACH, D), BF16),
             pltpu.VMEM((SHARD_ROWS, D), BF16),
-        ),
-        in_specs=[anywhere] * 6,
-        out_specs=(pl.BlockSpec(memory_space=pltpu.VMEM),) * 3,
+        )
+        + (pltpu.VMEM((SHARD_ROWS, D), F32),) * 4,
+        in_specs=[anywhere] * 8,
+        out_specs=(pl.BlockSpec(memory_space=pltpu.VMEM),) * 7,
         scratch_shapes=[
             vmem((4, TOKENS, 384), BF16),
             vmem((TOKENS, D), BF16),
-            vmem((SHARD_ROWS, D), F32),
             vmem((SHARD_ROWS, D), F32),
             vmem((TEACH, D), BF16),
             vmem((TEACH, D), BF16),
@@ -447,29 +461,23 @@
             vmem((TEACH, D), F32),
             pltpu.SemaphoreType.DMA((N_COPIES,)),
             pltpu.SemaphoreType.DMA((N_COPIES,)),
-            pltpu.SemaphoreType.DMA((9,)),
+            pltpu.SemaphoreType.DMA((11,)),
         ],
         compiler_params=pltpu.CompilerParams(
-            collective_id=0, has_side_effects=True, vmem_limit_bytes=54 * 2**20
+            collective_id=0, has_side_effects=True, vmem_limit_bytes=50 * 2**20
         ),
         cost_estimate=pl.CostEstimate(
             flops=2 * D * D * (2 * TOKENS + TEACH), bytes_accessed=22 * 2**20, transcendentals=0
         ),
         name="exchange",
-    )(student_ctx, out_grad, weight, teacher, teach_input, teach_ctx)
+    )(*operands)
 
 
 def finish_kernel(
-    ctx_grad, teacher_out, gradient, weight, moment_one, moment_two, teacher,
+    ctx_grad, teacher_out, gradient, weight, moment_one, moment_two, teacher_next,
     ctx_grad_o, weight_o, moment_one_o, moment_two_o, teacher_o, teacher_out_o,
-    w_v, one_v, two_v, t_v, wo_v, oneo_v, twoo_v, to_v, in_sem, out_sem,
+    wo_v, oneo_v, twoo_v, out_sem,
 ):
-    loads = [
-        pltpu.make_async_copy(src, dst, in_sem.at[i])
-        for i, (src, dst) in enumerate([(weight, w_v), (moment_one, one_v), (moment_two, two_v), (teacher, t_v)])
-    ]
-    for load in loads:
-        load.start()
     stores = []
 
     def store(src, dst):
@@ -477,33 +485,31 @@
         copy.start()
         stores.append(copy)
 
+    store(teacher_next, teacher_o)
     for r in range(4):
         rows = pl.ds(r * (TOKENS // 4), TOKENS // 4)
         store(ctx_grad.at[rows], ctx_grad_o.at[rows])
     for r in range(2):
         rows = pl.ds(r * (TEACH // 2), TEACH // 2)
         store(teacher_out.at[rows], teacher_out_o.at[rows])
-    for load in loads:
-        load.wait()
     correct_one = 1.0 - beta_one**STEP
     correct_two = 1.0 - beta_two**STEP
     for r in range(4):
         rows = pl.ds(r * BLOCK, BLOCK)
-        g, w = gradient[rows, :].astype(F32), w_v[rows, :]
-        one = beta_one * one_v[rows, :] + (1.0 - beta_one) * g
-        two = beta_two * two_v[rows, :] + (1.0 - beta_two) * g * g
+        g, w = gradient[rows, :].astype(F32), weight[rows, :]
+        one = beta_one * moment_one[rows, :] + (1.0 - beta_one) * g
+        two = beta_two * moment_two[rows, :] + (1.0 - beta_two) * g * g
         update = one / correct_one / (jnp.sqrt(two / correct_two) + adam_eps) + decay_rate * w
         wo_v[rows, :] = w - learn_rate * update
         oneo_v[rows, :] = one
         twoo_v[rows, :] = two
-        to_v[rows, :] = momentum * t_v[rows, :] + (1.0 - momentum) * w
-        for src, dst in ((wo_v, weight_o), (oneo_v, moment_one_o), (twoo_v, moment_two_o), (to_v, teacher_o)):
+        for src, dst in ((wo_v, weight_o), (oneo_v, moment_one_o), (twoo_v, moment_two_o)):
             store(src.at[rows], dst.at[rows])
     for copy in stores:
         copy.wait()
 
 
-def finish(ctx_grad, teacher_out, gradient, weight, moment_one, moment_two, teacher):
+def finish(*operands):
     anywhere, near = pl.BlockSpec(memory_space=pl.ANY), pl.BlockSpec(memory_space=pltpu.VMEM)
     state = jax.ShapeDtypeStruct((SHARD_ROWS, D), F32)
     return pl.pallas_call(
@@ -512,21 +518,20 @@
             jax.ShapeDtypeStruct((TOKENS, D), BF16), state, state, state, state,
             jax.ShapeDtypeStruct((TEACH, D), BF16),
         ),
-        in_specs=[near] * 3 + [anywhere] * 4,
+        in_specs=[near] * 7,
         out_specs=(anywhere,) * 6,
-        scratch_shapes=[pltpu.VMEM((SHARD_ROWS, D), F32)] * 8
-        + [pltpu.SemaphoreType.DMA((4,)), pltpu.SemaphoreType.DMA((22,))],
+        scratch_shapes=[pltpu.VMEM((SHARD_ROWS, D), F32)] * 3 + [pltpu.SemaphoreType.DMA((19,))],
         compiler_params=pltpu.CompilerParams(vmem_limit_bytes=24 * 2**20),
-        cost_estimate=pl.CostEstimate(flops=10 * SHARD_ROWS * D, bytes_accessed=16 * 2**20, transcendentals=0),
+        cost_estimate=pl.CostEstimate(flops=10 * SHARD_ROWS * D, bytes_accessed=12 * 2**20, transcendentals=0),
         name="finish",
-    )(ctx_grad, teacher_out, gradient, weight, moment_one, moment_two, teacher)
+    )(*operands)
 
 
 def body(student_ctx, out_grad, weight, moment_one, moment_two, teacher, teach_input, teach_ctx):
-    ctx_grad, teacher_out, gradient = communicate(
-        student_ctx, out_grad, weight, teacher, teach_input, teach_ctx
+    results = communicate(
+        student_ctx, out_grad, weight, moment_one, moment_two, teacher, teach_input, teach_ctx
     )
-    return finish(ctx_grad, teacher_out, gradient, weight, moment_one, moment_two, teacher)
+    return finish(*results)
 
 
 def solution(mesh):

time: 66.4 us -> 63 us (0.949)
  Pallas kernels: 63.9 us -> 61.9 us
  local copies, waits for them, and re-layouts: 1.28 us -> 0 us
    unnamed x8 -> x0, local copies, waits for them, and re-layouts: 1.28 us -> none
    pallas_call x1, Pallas kernels: 5.01 us -> 4.01 us  [finish(): pl.pallas_call(finish_kernel, out_shape=(jax.ShapeDtypeStruct((TOKENS, D)...]
    pallas_call x1, Pallas kernels: 58.9 us -> 57.9 us  [communicate(): pl.pallas_call(kernel, out_shape=(pltpu.VMEM((TOKENS, D), BF16), pltpu.VM...]
where the time goes in v3:
time: 63 us; the launch traced here: 62.7 us
  Pallas kernels  61.9 us (98%)
  between operations  0.8 us (1%)
    pallas_call x1, Pallas kernels, communicate(): pl.pallas_call(kernel, out_shape=(pltpu.VMEM((TOKENS, D), BF16), pltpu.VM...  57.9 us
    pallas_call x1, Pallas kernels, finish(): pl.pallas_call(finish_kernel, out_shape=(jax.ShapeDtypeStruct((TOKENS, D)...  4.01 us

profile of v3, /device:TPU:0, one launch (start us, length us, event | category | flops | bytes accessed | tf_op | source)
XLA Modules:
  0.0 62.7 jit_solution(6548675723421218159)
XLA Ops:
  0.6 57.9 %exchange.1 = (bf16[1280,1536]{1,0:T(8,128)(2,1)S(1)}, bf16[512,1536]{1,0:T(8,128)(2,1)S(1)}, bf16[192,1536]{1,0:T(8,128)(2,1)S(1)}, f32[192,1536]{1,0:T(8,128)S...) custom-call(bf16[1280,1536]{1,0:T(8,128)(2,1)} %student_ctx.1, ...), custom_call_target="tpu_custom_call" | custom-call | flops 14495514624 | bytes 23068672 | tf_op jit(solution)/shard_map/exchange/pallas_call | solution.py:422
  58.5 4.0 %finish.1 = (bf16[1280,1536]{1,0:T(8,128)(2,1)}, f32[192,1536]{1,0:T(8,128)}, f32[192,1536]{1,0:T(8,128)}, f32[192,1536]{1,0:T(8,128)}, f32[192,1536]{1,0:T(8,128)}, /*index=5*/bf16[512,1536]{1,0:T(8,128)(2,1)}) custom-call(bf16[1280,1536]{1,0:T(8,128)(2,1)S(1)} %get-tuple-element.13.ctx_grad, bf16[512,1536]{1,0:T(8,128)(2,1)S(1)} %get-tuple-element.14.teacher_out, ...), custom_call_target="tpu_custom_call" | custom-call | flops 2949120 | bytes 12582912 | tf_op jit(solution)/shard_map/finish/pallas_call | solution.py:515

commit v4 on v3

--- a/solution.py
+++ b/solution.py
@@ -367,8 +367,8 @@
     phase_one(2)
     grad_own(3)
     x_event_second()
+    phase_one(3)
     opposite_event()
-    phase_one(3)
     pass_on("X1", 4, half(0, False), right)
     pass_on("X1", 5, half(0, False), left)
     first_y(0)

time: 63 us -> 62.9 us (level)
  no operation moved by 1% of the time
where the time goes in v4:
time: 62.9 us; the launch traced here: 62.8 us
  Pallas kernels  62 us (99%)
  between operations  0.8 us (1%)
    pallas_call x1, Pallas kernels, communicate(): pl.pallas_call(kernel, out_shape=(pltpu.VMEM((TOKENS, D), BF16), pltpu.VM...  58 us
    pallas_call x1, Pallas kernels, finish(): pl.pallas_call(finish_kernel, out_shape=(jax.ShapeDtypeStruct((TOKENS, D)...  4.01 us

profile of v4, /device:TPU:0, one launch (start us, length us, event | category | flops | bytes accessed | tf_op | source)
XLA Modules:
  0.0 62.8 jit_solution(858006507658704626)
XLA Ops:
  0.6 58.0 %exchange.1 = (bf16[1280,1536]{1,0:T(8,128)(2,1)S(1)}, bf16[512,1536]{1,0:T(8,128)(2,1)S(1)}, bf16[192,1536]{1,0:T(8,128)(2,1)S(1)}, f32[192,1536]{1,0:T(8,128)S...) custom-call(bf16[1280,1536]{1,0:T(8,128)(2,1)} %student_ctx.1, ...), custom_call_target="tpu_custom_call" | custom-call | flops 14495514624 | bytes 23068672 | tf_op jit(solution)/shard_map/exchange/pallas_call | solution.py:422
  58.7 4.0 %finish.1 = (bf16[1280,1536]{1,0:T(8,128)(2,1)}, f32[192,1536]{1,0:T(8,128)}, f32[192,1536]{1,0:T(8,128)}, f32[192,1536]{1,0:T(8,128)}, f32[192,1536]{1,0:T(8,128)}, /*index=5*/bf16[512,1536]{1,0:T(8,128)(2,1)}) custom-call(bf16[1280,1536]{1,0:T(8,128)(2,1)S(1)} %get-tuple-element.13.ctx_grad, bf16[512,1536]{1,0:T(8,128)(2,1)S(1)} %get-tuple-element.14.teacher_out, ...), custom_call_target="tpu_custom_call" | custom-call | flops 2949120 | bytes 12582912 | tf_op jit(solution)/shard_map/finish/pallas_call | solution.py:515
